TPU v7x, 32 devices: a whole 2x2x4 slice. The times are simulated.
32 devices in a mesh: scenes: 2 (over x), rows: 16 (over z, y, core).
Axes of the slice: x: 2, y: 2, z: 4, core: 2. Of those that a mesh axis runs over, the one named last changes fastest.
Arguments:
- images: float32 [64, 128, 128], P(('scenes', 'rows')), parts along dimension 0, may hold values from -6 to 6
- conv_weight: float32 [3, 3, 128, 128], replicated, may hold values from -0.1875 to 0.1875
- lift_weight: float32 [320, 128], replicated, may hold values from -0.5 to 0.5
- vol_weight: float32 [3, 3, 3, 32, 40], replicated, may hold values from -0.1875 to 0.1875
Outputs:
- filtered: float32 [64, 32, 48, 128], P(('scenes', 'rows')), parts along dimension 0
There are 2 independent parts, one for each index of `scenes`. A program takes and returns all parts, laid end to end along the dimension named above; an argument that names none is the same for every part. Nothing has to cross between parts.
All inputs are finite; a program needn't handle non-finite values.
Results may differ from a plain program's by a relative error of at most 0.0001.
Values sent between devices are 32-bit elements; how exact they have to be, the bound alone decides.
No kernel may reach another device: no remote copies, remote signals or barrier semaphores. Data moves between devices by JAX's collectives and lax.ppermute only.
A program may use at most 128 MiB of HBM per device.

v0:
```python
import jax
import jax.numpy as jnp
from jax import lax
from jax.sharding import PartitionSpec as P

GROUPS = 40
DISP = 48


precise = lax.Precision.HIGHEST


def with_halo(x, sides, width):
    for axis, dim in sides:
        size, length = (lax.axis_size(axis), x.shape[dim])
        up = [(i, (i + 1) % size) for i in range(size)]
        down = [(j, i) for i, j in up]
        last = lax.slice_in_dim(x, length - width, length, axis=dim)
        first = lax.slice_in_dim(x, 0, width, axis=dim)
        before = lax.ppermute(last, axis, up)
        after = lax.ppermute(first, axis, down)
        x = jnp.concatenate([before, x, after], axis=dim)
    return x


def passed_along(x, axis, by):
    size = lax.axis_size(axis)
    return lax.ppermute(x, axis, [(i, (i + by) % size) for i in range(size)])


def conv_plane(planes, weight, padding):
    result = lax.conv_general_dilated(
        planes[None],
        weight,
        (1, 1),
        padding,
        dimension_numbers=("NHCW", "HWOI", "NHCW"),
        precision=precise,
    )
    return result[0]


def lift_features(weight, hidden):
    return jnp.einsum("fi,ric->rfc", weight, hidden, precision=precise)


def correlate(anchor, other, groups, disparities):
    row_count, channels, columns = anchor.shape
    padded = jnp.pad(other, ((0, 0), (0, 0), (disparities, 0)))
    layers = []
    for offset in range(disparities):
        shifted = padded[:, :, disparities - offset : disparities - offset + columns]
        product = (anchor * shifted).reshape(row_count, groups, channels // groups, columns)
        layers.append(jnp.mean(product, axis=2))
    return jnp.stack(layers, axis=2)


def conv_volume(volume, weight, padding):
    result = lax.conv_general_dilated(
        volume[None],
        weight,
        (1, 1, 1),
        padding,
        dimension_numbers=("NHCDW", "HDWOI", "NHCDW"),
        precision=precise,
    )
    return result[0]


def clip_rim(padded, axis_dim, position, quarter):
    extent = padded.shape[axis_dim]
    place = jnp.arange(extent)
    starts = (position == quarter) | (position == 3 * quarter)
    ends = (position == quarter - 1) | (position == 3 * quarter - 1)
    dropped = (place == 0) & starts | (place == extent - 1) & ends
    mask_shape = [1] * padded.ndim
    mask_shape[axis_dim] = extent
    return padded * jnp.where(dropped, 0.0, 1.0).astype(padded.dtype).reshape(mask_shape)


def on_device(images, conv_weight, lift_weight, vol_weight):
    devices = lax.axis_size("rows")
    position = lax.axis_index("rows")
    halfway = devices // 2
    quarter = devices // 4
    framed = with_halo(images, (("rows", 0),), 1)
    framed = clip_rim(framed, 0, position, quarter)
    hidden = jax.nn.relu(conv_plane(framed, conv_weight, ((0, 0), (1, 1))))
    features = lift_features(lift_weight, hidden)
    partner = lift_features(lift_weight, passed_along(hidden, "rows", halfway))
    is_right = (position < quarter) | (position >= 3 * quarter)

    def orient(values):
        return jnp.where(is_right, jnp.flip(values, -1), values)

    volume = orient(correlate(orient(features), orient(partner), GROUPS, DISP))
    volume = with_halo(volume, (("rows", 0),), 1)
    volume = clip_rim(volume, 0, position, quarter)
    return conv_volume(volume, vol_weight, ((0, 0), (1, 1), (1, 1)))


def solution(mesh):
    placed = (P(("scenes", "rows"), None, None), P(), P(), P())
    return jax.shard_map(
        on_device,
        mesh=mesh,
        in_specs=placed,
        out_specs=P(("scenes", "rows"), None, None, None),
        check_vma=False,
    )
```

profile of v0, /device:TPU:1, one launch (start us, length us, event | category | flops | bytes accessed | tf_op | source)
XLA Modules:
  0.0 253.1 jit_solution(3526295873962544792)
XLA Ops:
  0.0 0.9 fusion.168
  1.0 2.7 %collective-permute-start = (f32[1,128,128]{2,1,0:T(8,128)S(1)}, f32[1,128,128]{2,1,0:T(8,128)S(1)}, u32[]{:S(2)}, u32[]{:S(2)}) collective-permute-start(f32[1,128,128]{2,1,0:T(8,128)S(1)} %get-tuple-element.56), channel_id=1, source_target_pairs={{0,1},{1,2},{2,3},{3,4},{4,5},{5,6},{6,7},{7,8},{8,9},{9,10},{10,1... | collective-permute-start | bytes 196616 | tf_op jit(solution)/shard_map/ppermute | solution.py:20
  3.6 1.3 collective-permute-done
  5.0 3.1 %collective-permute-done.1 = f32[1,128,128]{2,1,0:T(8,128)S(1)} collective-permute-done((f32[1,128,128]{2,1,0:T(8,128)S(1)}, f32[1,128,128]{2,1,0:T(8,128)S(1)}, u32[]{:S(2)}, u32[]{:S(2)}) %collective-permute-start.1) | collective-permute-done | bytes 65568 | tf_op jit(solution)/shard_map/ppermute | solution.py:21
  8.1 1.0 fusion.156
  9.4 1.2 fusion.10
  10.7 1.6 collective-permute-start.2
  13.7 6.0 %collective-permute-done.2 = f32[2,128,128]{2,1,0:T(8,128)S(1)} collective-permute-done((f32[2,128,128]{2,1,0:T(8,128)S(1)}, f32[2,128,128]{2,1,0:T(8,128)S(1)}, u32[]{:S(2)}, u32[]{:S(2)}) %collective-permute-start.2) | collective-permute-done | bytes 131104 | tf_op jit(solution)/shard_map/ppermute | solution.py:28
  21.0 1.9 fusion.151
  22.9 1.2 fusion.43
  24.1 1.8 fusion.97
  26.6 2.5 %rev.13 = f32[2,40,48,128]{3,1,0,2:T(8,128)} reverse(f32[2,40,48,128]{3,1,0,2:T(8,128)S(1)} %constant_dynamic-update-slice_fusion), dimensions={3} | reverse | bytes 3932160 | tf_op jit(solution)/shard_map/jit(_flip)/rev | solution.py:94
  29.2 1.8 broadcast_select_fusion.1
  32.0 20.8 %collective-permute-done.3 = f32[1,40,48,128]{3,1,2,0:T(8,128)S(1)} collective-permute-done((f32[1,40,48,128]{3,1,2,0:T(8,128)S(1)}, f32[1,40,48,128]{3,1,2,0:T(8,128)S(1)}, u32[]{:S(2)}, u32[]{:S(2)}) %collective-permute-start.3) | collective-permute-done | bytes 983072 | tf_op jit(solution)/shard_map/ppermute | solution.py:20
  52.7 2.5 %collective-permute-done.4 = f32[1,40,48,128]{3,1,0,2:T(8,128)S(1)} collective-permute-done((f32[1,40,48,128]{3,1,0,2:T(8,128)S(1)}, f32[1,40,48,128]{3,1,0,2:T(8,128)S(1)}, u32[]{:S(2)}, u32[]{:S(2)}) %collective-permute-start.4) | collective-permute-done | bytes 983072 | tf_op jit(solution)/shard_map/ppermute | solution.py:21
  55.3 2.6 %fusion.7 = f32[4,40,48,1,128]{4,1,0,2,3:T(8,128)} fusion(f32[1,1,40,48,128]{4,2,1,3,0:T(8,128)S(1)} %bitcast.341, f32[1,2,40,48,128]{4,2,1,3,0:T(8,128)S(1)} %bitcast.337, f32[1,1,40,48,128]{4,2,1,3,0:T(8,128)S(1)} %bitcast.340, f32[4]{0:T(128)S(1)} %or_select_fusion), kind=kLoop, calls=%fused_computation.57 | loop fusion | flops 2949120 | bytes 7864336 | tf_op jit(solution)/shard_map/mul | solution.py:78
  57.8 8.2 %copy.123 = f32[4,40,48,1,128]{2,1,4,0,3:T(8,128)} copy(f32[4,40,48,1,128]{4,1,0,2,3:T(8,128)} %fusion.7) | data formatting | bytes 7864320
  66.1 8.8 %pad.7.clone = f32[4,40,48,1,136]{2,1,4,0,3:T(8,128)} pad(f32[4,40,48,1,128]{2,1,4,0,3:T(8,128)} %copy.123, f32[]{:T(128)} %constant.70.clone.1), padding=0_0x0_0x0_0x0_0x1_7 | pad | bytes 8110084 | tf_op jit(solution)/shard_map/mul | solution.py:78
  74.9 14.0 %copy.117 = f32[4,40,48,1,8,17]{1,4,5,2,0,3:T(8,128)} copy(f32[4,40,48,1,8,17]{2,1,5,4,0,3:T(8,128)} %bitcast.336) | data formatting | bytes 8355840 | tf_op jit(solution)/shard_map/conv_general_dilated | solution.py:59
  88.8 1.6 slice.213
  90.5 147.0 %broadcast_select_fusion = f32[2,48,8,17,32]{4,2,3,1,0:T(8,128)} fusion(pred[8,17]{0,1:T(8,128)(4,1)S(1)} %copy-done.3, f32[3,3,3,32,40]{4,3,2,1,0:T(8,128)S(1)} %copy-done.4, f32[4,40,48,1,7,2]{1,4,5,2,0,3:T(8,128)S(1)} %slice.213, f32[4,40,48,1,8,17]{1,4,5,2,0,3:T(8,128)} %copy.117), kind=kOutput, calls=%fused_computation.58 | convolution fusion | flops 5343301632 | bytes 6417544 | tf_op jit(solution)/shard_map/conv_general_dilated | solution.py:59
  237.5 6.4 %copy.118 = f32[2,48,8,17,32]{1,4,3,2,0:T(8,128)} copy(f32[2,48,8,17,32]{4,2,3,1,0:T(8,128)} %broadcast_select_fusion) | data formatting | bytes 3342336 | tf_op jit(solution)/shard_map/conv_general_dilated | solution.py:59
  243.9 4.7 %slice_bitcast_fusion = f32[2,32,48,128]{2,1,3,0:T(8,128)} fusion(f32[2,48,1,136,32]{1,4,3,0,2:T(8,128)} %bitcast.338), kind=kLoop, calls=%fused_computation.55 | loop fusion | bytes 3145728 | tf_op jit(solution)/shard_map/squeeze | solution.py:67
  248.5 4.6 %copy.119 = f32[2,32,48,128]{3,2,1,0:T(8,128)} copy(f32[2,32,48,128]{2,1,3,0:T(8,128)} %slice_bitcast_fusion) | data formatting | bytes 3145728 | tf_op jit(solution)/shard_map/squeeze | solution.py:67
  (75 shorter events, 4.3 us)
Async XLA Ops:
  0.0 9.4 %copy-start = (f32[3,3,128,128]{3,2,1,0:T(8,128)S(1)}, f32[3,3,128,128]{3,2,1,0:T(8,128)}, u32[]{:S(2)}) copy-start(f32[3,3,128,128]{3,2,1,0:T(8,128)} %param.5) | copy-start | bytes 1769476
  0.0 9.4 %copy-start.3 = (pred[8,17]{0,1:T(8,128)(4,1)S(1)}, pred[8,17]{0,1:T(8,128)(4,1)}, u32[]{:S(2)}) copy-start(pred[8,17]{0,1:T(8,128)(4,1)} %constant.84) | copy-start | bytes 412
  1.0 4.0 %collective-permute-start = (f32[1,128,128]{2,1,0:T(8,128)S(1)}, f32[1,128,128]{2,1,0:T(8,128)S(1)}, u32[]{:S(2)}, u32[]{:S(2)}) collective-permute-start(f32[1,128,128]{2,1,0:T(8,128)S(1)} %get-tuple-element.56), channel_id=1, source_target_pairs={{0,1},{1,2},{2,3},{3,4},{4,5},{5,6},{6,7},{7,8},{8,9},{9,10},{10,1... | collective-permute-start | bytes 196616 | tf_op jit(solution)/shard_map/ppermute | solution.py:20
  3.6 4.4 %collective-permute-start.1 = (f32[1,128,128]{2,1,0:T(8,128)S(1)}, f32[1,128,128]{2,1,0:T(8,128)S(1)}, u32[]{:S(2)}, u32[]{:S(2)}) collective-permute-start(f32[1,128,128]{2,1,0:T(8,128)S(1)} %get-tuple-element.57), channel_id=1, source_target_pairs={{1,0},{2,1},{3,2},{4,3},{5,4},{6,5},{7,6},{8,7},{9,8},{10,9},{11,1... | collective-permute-start | bytes 196616 | tf_op jit(solution)/shard_map/ppermute | solution.py:21
  8.1 4.3 %copy-start.2 = (f32[320,128]{1,0:T(8,128)S(1)}, f32[320,128]{1,0:T(8,128)}, u32[]{:S(2)}) copy-start(f32[320,128]{1,0:T(8,128)} %param.6) | copy-start | bytes 491524
  10.7 8.9 %collective-permute-start.2 = (f32[2,128,128]{2,1,0:T(8,128)S(1)}, f32[2,128,128]{2,1,0:T(8,128)S(1)}, u32[]{:S(2)}, u32[]{:S(2)}) collective-permute-start(f32[2,128,128]{2,1,0:T(8,128)S(1)} %bitcast.344), channel_id=1, source_target_pairs={{0,8},{1,9},{2,10},{3,11},{4,12},{5,13},{6,14},{7,15},{8,0},{9,1},... | collective-permute-start | bytes 393224 | tf_op jit(solution)/shard_map/ppermute | solution.py:28
  31.1 21.6 %collective-permute-start.3 = (f32[1,40,48,128]{3,1,2,0:T(8,128)S(1)}, f32[1,40,48,128]{3,1,2,0:T(8,128)S(1)}, u32[]{:S(2)}, u32[]{:S(2)}) collective-permute-start(f32[1,40,48,128]{3,1,2,0:T(8,128)S(1)} %get-tuple-element.54), channel_id=1, source_target_pairs={{0,1},{1,2},{2,3},{3,4},{4,5},{5,6},{6,7},{7,8},{8,9},{9,10},{10,1... | collective-permute-start | bytes 2949128 | tf_op jit(solution)/shard_map/ppermute | solution.py:20
  31.2 24.1 %collective-permute-start.4 = (f32[1,40,48,128]{3,1,0,2:T(8,128)S(1)}, f32[1,40,48,128]{3,1,0,2:T(8,128)S(1)}, u32[]{:S(2)}, u32[]{:S(2)}) collective-permute-start(f32[1,40,48,128]{3,1,0,2:T(8,128)S(1)} %get-tuple-element.55), channel_id=1, source_target_pairs={{1,0},{2,1},{3,2},{4,3},{5,4},{6,5},{7,6},{8,7},{9,8},{10,9},{11,1... | collective-permute-start | bytes 2949128 | tf_op jit(solution)/shard_map/ppermute | solution.py:21
  88.8 1.7 copy-start.4
  243.9 9.3 %copy-start.1 = (f32[3,3,128,128]{3,2,1,0:T(8,128)S(1)}, f32[3,3,128,128]{3,2,1,0:T(8,128)}, u32[]{:S(2)}) copy-start(f32[3,3,128,128]{3,2,1,0:T(8,128)} %param.5) | copy-start | bytes 1769476
where the time goes:
time: 254 us; the launch traced here: 253 us
  matrix products  149 us (59%)
  local copies, waits for them, and re-layouts  54 us (21%)
  waiting for transfers between devices  33.7 us (13%)
  other arithmetic  10.7 us (4%)
  starting transfers between devices  5.2 us (2%)
    conv_general_dilated x1, matrix products, conv_volume(): lax.conv_general_dilated(volume[None], weight, (1, 1, 1), padding, dimens...  147 us
    ppermute x2, waiting for transfers between devices, with_halo(): before = lax.ppermute(last, axis, up)  22.1 us
    conv_general_dilated x3, local copies, waits for them, and re-layouts, conv_volume(): lax.conv_general_dilated(volume[None], weight, (1, 1, 1), padding, dimens...  22 us
    squeeze x2, local copies, waits for them, and re-layouts, conv_volume(): return result[0]  9.29 us
    mul x2, local copies, waits for them, and re-layouts, clip_rim(): padded * jnp.where(dropped, 0.0, 1.0).astype(padded.dtype).reshape(mask_s...  8.84 us
    unnamed x14, local copies, waits for them, and re-layouts  8.62 us
    ppermute x1, waiting for transfers between devices, passed_along(): return lax.ppermute(x, axis, [(i, (i + by) % size) for i in range(size)])  5.98 us
    ppermute x2, waiting for transfers between devices, with_halo(): after = lax.ppermute(first, axis, down)  5.64 us
  transfers between devices with their start and end apart: 5, of which 5 were waited for; matrix products, arithmetic and copies ran while one was open for 1% of the time, Pallas kernels for 0%

commit v1 on v0

v1 whole, which is shorter than its diff:
```python
import functools

import jax
import jax.numpy as jnp
from jax import lax
from jax.experimental import pallas as pl
from jax.experimental.pallas import tpu as pltpu
from jax.sharding import PartitionSpec as P

GROUPS = 40
DISP = 48
F32 = jnp.float32
BF16 = jnp.bfloat16
VMEM_BYTES = 48 * 1024 * 1024


def split(x):
    high = x.astype(BF16)
    return high, (x - high.astype(F32)).astype(BF16)


def split_outside(x):
    high = lax.reduce_precision(x, 8, 7)
    return high.astype(BF16), (x - high).astype(BF16)


def mm(a, b):
    return jnp.dot(a, b, preferred_element_type=F32)


def from_columns(y, size):
    column = lax.broadcasted_iota(jnp.int32, (size, y.shape[1]), 1)
    last = y.shape[1] - 1
    left = jnp.where(column > 0, pltpu.roll(y[:size], 1, 1), 0.0)
    right = jnp.where(column < last, pltpu.roll(y[2 * size :], last, 1), 0.0)
    return y[size : 2 * size] + left + right


def features_kernel(flags, own, mate, far, conv_high, conv_low, lift_high, lift_low, out, x_high, x_low):
    rows, channels, columns = own.shape
    edge = mate.shape[0]
    odd = flags[0]
    total = rows + 2 * edge

    def place(block, at):
        count = block.shape[0] * channels
        high, low = split(block[...].reshape(count, columns))
        x_high[pl.ds(pl.multiple_of(at * channels, channels), count)] = high
        x_low[pl.ds(pl.multiple_of(at * channels, channels), count)] = low

    place(own, edge)
    place(mate, jnp.where(odd == 1, 0, total - edge))
    place(far, jnp.where(odd == 1, total - edge, 0))
    depth = 3 * channels
    feats = lift_high.shape[0]
    for row in range(0, rows + 2, 2):
        starts = [(row + k) * channels for k in range(2)]
        high = jnp.concatenate([x_high[s : s + depth] for s in starts], axis=1)
        low = jnp.concatenate([x_low[s : s + depth] for s in starts], axis=1)
        y = mm(conv_high[...], high) + (mm(conv_low[...], high) + mm(conv_high[...], low))
        hidden = []
        for k in range(2):
            h = jnp.maximum(from_columns(y[:, k * columns : (k + 1) * columns], channels), 0.0)
            if row + k == 0:
                h = h * flags[1].astype(F32)
            if row + k == rows + 1:
                h = h * flags[2].astype(F32)
            hidden.append(h)
        high, low = split(jnp.concatenate(hidden, axis=1))
        f = mm(lift_high[...], high) + (mm(lift_low[...], high) + mm(lift_high[...], low))
        for k in range(2):
            out[(row + k) * feats : (row + k + 1) * feats] = f[:, k * columns : (k + 1) * columns]


def volume_kernel(flags, anchor, other, weight, out, cost, c_high, c_low, *, rows, outs):
    columns = anchor.shape[1]
    slab = (rows + 2) * GROUPS
    per = anchor.shape[0] // slab
    right = flags[3] == 1
    column = lax.broadcasted_iota(jnp.int32, (8, columns), 1)
    place = jnp.where(right, columns - 1 - column, column)
    cost[:slab] = jnp.zeros((slab, columns), F32)
    cost[(DISP + 1) * slab :] = jnp.zeros((slab, columns), F32)

    def correlate(i, carry):
        at = pl.ds(pl.multiple_of(i * 8 * per, 8 * per), 8 * per)
        a = anchor[at]
        b = other[at]
        for d in range(DISP):
            shifted = pltpu.roll(b, jnp.where(right, columns - d, d), 1) if d else b
            c = jnp.sum((a * shifted).reshape(per, 8, columns), axis=0)
            if d:
                c = jnp.where(place >= d, c, 0.0)
            cost[pl.ds(pl.multiple_of((d + 1) * slab + i * 8, 8), 8)] = c
        return carry

    lax.fori_loop(0, slab // 8, correlate, 0)

    def halve(d, carry):
        at = pl.ds(pl.multiple_of(d * slab, slab), slab)
        high, low = split(cost[at])
        c_high[at] = high
        c_low[at] = low
        return carry

    lax.fori_loop(0, DISP + 2, halve, 0)
    m = 3 * rows * outs

    def filter_two(q, carry):
        base = q * 2 * slab
        ats = [pl.ds(pl.multiple_of(base + k * slab, slab), 3 * slab) for k in range(2)]
        high = jnp.concatenate([c_high[at] for at in ats], axis=1)
        low = jnp.concatenate([c_low[at] for at in ats], axis=1)
        y = mm(weight[...], high)
        y = y[:m] + (y[m:] + mm(weight[:m], low))
        for k in range(2):
            o = from_columns(y[:, k * columns : (k + 1) * columns], rows * outs)
            out[pl.ds(2 * q + k, rows * outs, stride=DISP)] = o
        return carry

    lax.fori_loop(0, DISP // 2, filter_two, 0)


def vmem():
    return pl.BlockSpec(memory_space=pltpu.VMEM)


def smem():
    return pl.BlockSpec(memory_space=pltpu.SMEM)


def features(flags, own, mate, far, conv, lift):
    rows, channels, columns = own.shape
    total = (rows + 2 * mate.shape[0]) * channels
    return pl.pallas_call(
        features_kernel,
        out_shape=jax.ShapeDtypeStruct(((rows + 2) * lift[0].shape[0], columns), F32),
        in_specs=[smem()] + [vmem()] * 7,
        out_specs=vmem(),
        scratch_shapes=[pltpu.VMEM((total, columns), BF16)] * 2,
        compiler_params=pltpu.CompilerParams(vmem_limit_bytes=VMEM_BYTES),
        name="features",
    )(flags, own, mate, far, *conv, *lift)


def volumes(flags, anchor, other, weight, rows, outs):
    columns = anchor.shape[1]
    depth = (DISP + 2) * (rows + 2) * GROUPS
    return pl.pallas_call(
        functools.partial(volume_kernel, rows=rows, outs=outs),
        out_shape=jax.ShapeDtypeStruct((rows * outs * DISP, columns), F32),
        in_specs=[smem()] + [vmem()] * 3,
        out_specs=vmem(),
        scratch_shapes=[pltpu.VMEM((depth, columns), F32), pltpu.VMEM((depth, columns), BF16), pltpu.VMEM((depth, columns), BF16)],
        compiler_params=pltpu.CompilerParams(vmem_limit_bytes=VMEM_BYTES),
        name="volumes",
    )(flags, anchor, other, weight)


def conv_operand(weight):
    outs, ins = weight.shape[2:]
    return split_outside(weight.transpose(1, 2, 0, 3).reshape(3 * outs, 3 * ins))


def lift_operand(weight):
    feats, ins = weight.shape
    per = feats // GROUPS
    ordered = weight.reshape(GROUPS // 8, 8, per, ins).transpose(0, 2, 1, 3)
    return split_outside(ordered.reshape(feats, ins))


def volume_operand(weight, rows, per):
    outs, groups = weight.shape[3:]
    taps = (weight * (1.0 / per)).transpose(2, 3, 1, 0, 4).reshape(3, outs, 3, 3 * groups)
    banded = [jnp.pad(taps, ((0, 0), (0, 0), (0, 0), (r * groups, (rows - 1 - r) * groups))) for r in range(rows)]
    whole = jnp.stack(banded, axis=1).reshape(3 * rows * outs, 3 * (rows + 2) * groups)
    return jnp.concatenate(split_outside(whole), axis=0)


def neighbours(size, quarter):
    def across(i):
        return (i + 1) % size if i % 2 else (i - 1) % size

    def apart(i):
        low, high = min(i, across(i)), max(i, across(i))
        return high - low == 1 and high in (quarter, 3 * quarter)

    mates = [(i, i ^ 1) for i in range(size)]
    far = [(i, across(i)) for i in range(size) if not apart(i)]
    return mates, far


def on_device(images, conv_weight, lift_weight, vol_weight):
    size = lax.axis_size("rows")
    position = lax.axis_index("rows")
    half, quarter = size // 2, size // 4
    rows = images.shape[0]
    odd = position % 2
    mates, far = neighbours(size, quarter)
    starts = (position == quarter) | (position == 3 * quarter)
    ends = (position == quarter - 1) | (position == 3 * quarter - 1)
    right = (position < quarter) | (position >= 3 * quarter)
    flags = jnp.stack([odd, jnp.where(starts, 0, 1), jnp.where(ends, 0, 1), jnp.where(right, 1, 0)]).astype(jnp.int32)

    def sent(x, to_first):
        if rows == 2:
            return x
        return jnp.where(to_first, x[:2], x[rows - 2 :])

    def framed(x):
        return lax.ppermute(sent(x, odd == 1), "rows", mates), lax.ppermute(sent(x, odd == 0), "rows", far)

    partner = lax.ppermute(images, "rows", [(i, (i + half) % size) for i in range(size)])
    conv = conv_operand(conv_weight)
    lift = lift_operand(lift_weight)
    per = lift_weight.shape[0] // GROUPS
    outs = vol_weight.shape[3]
    vol = volume_operand(vol_weight, rows, per)
    mine = features(flags, images, *framed(images), conv, lift)
    theirs = features(flags, partner, *framed(partner), conv, lift)
    result = volumes(flags, mine, theirs, vol, rows, outs)
    return result.reshape(rows, outs, DISP, images.shape[2])


def solution(mesh):
    return jax.shard_map(
        on_device,
        mesh=mesh,
        in_specs=(P(("scenes", "rows"), None, None), P(), P(), P()),
        out_specs=P(("scenes", "rows"), None, None, None),
        check_vma=False,
    )
```

time: 254 us -> 49 us (0.19)
  the two profiles are of different devices: /device:TPU:1 before, /device:TPU:0 now
where the time goes in v1:
time: 49 us; the launch traced here: 48.7 us
  Pallas kernels  27 us (55%)
  starting transfers between devices  11.7 us (24%)
  waiting for transfers between devices  5.41 us (11%)
  local copies, waits for them, and re-layouts  3.05 us (6%)
  other arithmetic  1.38 us (3%)
    pallas_call x1, Pallas kernels, volumes(): pl.pallas_call(functools.partial(volume_kernel, rows=rows, outs=outs), ou...  21.3 us
    ppermute x2, starting transfers between devices, framed(): lax.ppermute(sent(x, odd == 0), 'rows', far)  11.3 us
    pallas_call x2, Pallas kernels, features(): pl.pallas_call(features_kernel, out_shape=jax.ShapeDtypeStruct(((rows + 2...  5.67 us
    ppermute x1, waiting for transfers between devices, on_device(): lax.ppermute(images, 'rows', [(i, (i + half) % size) for i in range(size)])  3.49 us
    ppermute x2, waiting for transfers between devices, framed(): lax.ppermute(sent(x, odd == 0), 'rows', far)  1.91 us
    transpose x1, other arithmetic, volume_operand(): (weight * (1.0 / per)).transpose(2, 3, 1, 0, 4)  1.05 us
  transfers between devices with their start and end apart: 5, of which 2 were waited for; matrix products, arithmetic and copies ran while one was open for 9% of the time, Pallas kernels for 6%

profile of v1, /device:TPU:0, one launch (start us, length us, event | category | flops | bytes accessed | tf_op | source)
XLA Modules:
  0.0 48.7 jit_solution(2056234801159758155)
XLA Ops:
  0.0 7.3 %collective-permute-start.1 = (f32[2,128,128]{2,1,0:T(8,128)}, f32[2,128,128]{2,1,0:T(8,128)S(1)}, u32[]{:S(2)}, u32[]{:S(2)}) collective-permute-start(f32[2,128,128]{2,1,0:T(8,128)} %own.1), channel_id=1, source_target_pairs={{0,15},{1,2},{2,1},{5,6},{6,5},{7,8},{8,7},{9,10},{10,9},{13,14},{... | collective-permute-start | bytes 393224 | tf_op jit(solution)/shard_map/ppermute | solution.py:211
  7.4 0.1 collective-permute-start
  7.4 0.2 collective-permute-start.2
  7.6 0.9 %copy.9 = f32[5,8,8,128]{3,1,2,0:T(8,128)S(1)} copy(f32[5,8,8,128]{3,2,1,0:T(8,128)} %bitcast.27) | data formatting | bytes 327680 | tf_op jit(solution)/shard_map/reshape | solution.py:168
  8.6 1.0 %multiply_bitcast_fusion = f32[3,32,3,3,40]{4,1,0,2,3:T(8,128)S(1)} fusion(f32[3,3,3,32,40]{4,3,2,1,0:T(8,128)} %param.7), kind=kLoop, calls=%fused_computation.6 | loop fusion | flops 34560 | bytes 276480 | tf_op jit(solution)/shard_map/transpose | solution.py:174
  9.6 0.3 copy.10
  10.0 0.2 reshape.21
  10.2 0.1 pad_bitcast_fusion.1
  10.4 0.0 copy-start.1
  10.4 0.4 copy.11
  10.8 0.4 reshape.22
  11.3 0.2 copy-done.1
  11.5 0.4 copy.8
  11.9 0.0 copy-start
  11.9 0.1 fusion
  12.0 3.5 %collective-permute-done.2.own = f32[2,128,128]{2,1,0:T(8,128)S(1)} collective-permute-done((f32[2,128,128]{2,1,0:T(8,128)}, f32[2,128,128]{2,1,0:T(8,128)S(1)}, u32[]{:S(2)}, u32[]{:S(2)}) %collective-permute-start.2) | collective-permute-done | bytes 131104 | tf_op jit(solution)/shard_map/ppermute | solution.py:213
  15.5 4.0 %collective-permute-start.4 = (f32[2,128,128]{2,1,0:T(8,128)S(1)}, f32[2,128,128]{2,1,0:T(8,128)S(1)}, u32[]{:S(2)}, u32[]{:S(2)}) collective-permute-start(f32[2,128,128]{2,1,0:T(8,128)S(1)} %collective-permute-done.2.own), channel_id=1, source_target_pairs={{0,15},{1,2},{2,1},{5,6},{6,5},{7,8},{8,7},{9,10},{10,9},{13,14},{... | collective-permute-start | bytes 393224 | tf_op jit(solution)/shard_map/ppermute | solution.py:211
  19.5 0.1 collective-permute-start.3
  19.6 0.1 pad_add_fusion.flags
  19.7 0.0 collective-permute-done.1.far
  19.7 2.8 %features.2.anchor = f32[1280,128]{1,0:T(8,128)S(1)} custom-call(s32[4]{0:T(128)S(1)} %pad_add_fusion.flags, f32[2,128,128]{2,1,0:T(8,128)S(1)} %copy-done, f32[2,128,128]{2,1,0:T(8,128)S(1)} %collective-permute-done.mate, f32[2,128,128]{2,1,0:T(8,128)S(1)} %collective-permute-done.1.far, bf16[384,384]{1,0:T(8,128)(2,1)S(1)} %get-tuple-element.6.conv_high, ...), custom_call_target="tpu_custom_call" | custom-call | tf_op jit(solution)/shard_map/features/pallas_call | solution.py:135
  22.6 1.9 %collective-permute-done.4.far = f32[2,128,128]{2,1,0:T(8,128)S(1)} collective-permute-done((f32[2,128,128]{2,1,0:T(8,128)S(1)}, f32[2,128,128]{2,1,0:T(8,128)S(1)}, u32[]{:S(2)}, u32[]{:S(2)}) %collective-permute-start.4) | collective-permute-done | bytes 131104 | tf_op jit(solution)/shard_map/ppermute | solution.py:211
  24.5 2.8 %features.3.other = f32[1280,128]{1,0:T(8,128)S(1)} custom-call(s32[4]{0:T(128)S(1)} %pad_add_fusion.flags, f32[2,128,128]{2,1,0:T(8,128)S(1)} %collective-permute-done.2.own, f32[2,128,128]{2,1,0:T(8,128)S(1)} %collective-permute-done.3.mate, f32[2,128,128]{2,1,0:T(8,128)S(1)} %collective-permute-done.4.far, ...), custom_call_target="tpu_custom_call" | custom-call | tf_op jit(solution)/shard_map/features/pallas_call | solution.py:135
  27.3 21.3 %volumes.1 = f32[3072,128]{1,0:T(8,128)} custom-call(s32[4]{0:T(128)S(1)} %pad_add_fusion.flags, f32[1280,128]{1,0:T(8,128)S(1)} %features.2.anchor, f32[1280,128]{1,0:T(8,128)S(1)} %features.3.other, bf16[384,480]{1,0:T(8,128)(2,1)S(1)} %pad_maximum_fusion.1.weight), custom_call_target="tpu_custom_call" | custom-call | tf_op jit(solution)/shard_map/volumes/pallas_call | solution.py:149
  (7 shorter events, 0.2 us)
Async XLA Ops:
  0.0 19.7 %collective-permute-start.1 = (f32[2,128,128]{2,1,0:T(8,128)}, f32[2,128,128]{2,1,0:T(8,128)S(1)}, u32[]{:S(2)}, u32[]{:S(2)}) collective-permute-start(f32[2,128,128]{2,1,0:T(8,128)} %own.1), channel_id=1, source_target_pairs={{0,15},{1,2},{2,1},{5,6},{6,5},{7,8},{8,7},{9,10},{10,9},{13,14},{... | collective-permute-start | bytes 393224 | tf_op jit(solution)/shard_map/ppermute | solution.py:211
  7.4 12.4 %collective-permute-start = (f32[2,128,128]{2,1,0:T(8,128)}, f32[2,128,128]{2,1,0:T(8,128)S(1)}, u32[]{:S(2)}, u32[]{:S(2)}) collective-permute-start(f32[2,128,128]{2,1,0:T(8,128)} %own.1), channel_id=1, source_target_pairs={{0,1},{1,0},{2,3},{3,2},{4,5},{5,4},{6,7},{7,6},{8,9},{9,8},{10,11... | collective-permute-start | bytes 393224 | tf_op jit(solution)/shard_map/ppermute | solution.py:211
  7.4 8.1 %collective-permute-start.2 = (f32[2,128,128]{2,1,0:T(8,128)}, f32[2,128,128]{2,1,0:T(8,128)S(1)}, u32[]{:S(2)}, u32[]{:S(2)}) collective-permute-start(f32[2,128,128]{2,1,0:T(8,128)} %own.1), channel_id=1, source_target_pairs={{0,8},{1,9},{2,10},{3,11},{4,12},{5,13},{6,14},{7,15},{8,0},{9,1},... | collective-permute-start | bytes 393224 | tf_op jit(solution)/shard_map/ppermute | solution.py:213
  10.4 1.1 %copy-start.1 = (f32[3,3,128,128]{3,2,1,0:T(8,128)S(1)}, f32[3,3,128,128]{3,2,1,0:T(8,128)}, u32[]{:S(2)}) copy-start(f32[3,3,128,128]{3,2,1,0:T(8,128)} %param.5) | copy-start | bytes 1769476
  11.9 7.9 %copy-start = (f32[2,128,128]{2,1,0:T(8,128)S(1)}, f32[2,128,128]{2,1,0:T(8,128)}, u32[]{:S(2)}) copy-start(f32[2,128,128]{2,1,0:T(8,128)} %own.1) | copy-start | bytes 393220
  15.5 9.0 %collective-permute-start.4 = (f32[2,128,128]{2,1,0:T(8,128)S(1)}, f32[2,128,128]{2,1,0:T(8,128)S(1)}, u32[]{:S(2)}, u32[]{:S(2)}) collective-permute-start(f32[2,128,128]{2,1,0:T(8,128)S(1)} %collective-permute-done.2.own), channel_id=1, source_target_pairs={{0,15},{1,2},{2,1},{5,6},{6,5},{7,8},{8,7},{9,10},{10,9},{13,14},{... | collective-permute-start | bytes 393224 | tf_op jit(solution)/shard_map/ppermute | solution.py:211
  19.5 5.0 %collective-permute-start.3 = (f32[2,128,128]{2,1,0:T(8,128)S(1)}, f32[2,128,128]{2,1,0:T(8,128)S(1)}, u32[]{:S(2)}, u32[]{:S(2)}) collective-permute-start(f32[2,128,128]{2,1,0:T(8,128)S(1)} %collective-permute-done.2.own), channel_id=1, source_target_pairs={{0,1},{1,0},{2,3},{3,2},{4,5},{5,4},{6,7},{7,6},{8,9},{9,8},{10,11... | collective-permute-start | bytes 393224 | tf_op jit(solution)/shard_map/ppermute | solution.py:211

commit v2 on v0

v2 whole, which is shorter than its diff:
```python
import jax
import jax.numpy as jnp
from jax import lax
from jax.experimental import pallas as pl
from jax.experimental.pallas import tpu as pltpu
from jax.sharding import PartitionSpec as P

GROUPS = 40
DISP = 48
STEP = 8
COST = 10**11
F32 = jnp.float32
BF16 = jnp.bfloat16
VMEM_BYTES = 24 * 1024 * 1024


def split(x):
    high = x.astype(BF16)
    return high, (x - high.astype(F32)).astype(BF16)


def mm(a, b):
    return jnp.dot(a, b, preferred_element_type=F32)


def from_columns(y, size):
    column = lax.broadcasted_iota(jnp.int32, (size, y.shape[1]), 1)
    last = y.shape[1] - 1
    left = jnp.where(column > 0, pltpu.roll(y[:size], 1, 1), 0.0)
    right = jnp.where(column < last, pltpu.roll(y[2 * size :], last, 1), 0.0)
    return y[size : 2 * size] + left + right


def features(x, operands, to, inside):
    conv_high, conv_low, lift_high, lift_low = operands
    channels = conv_high.shape[0] // 3
    columns = x.shape[2]
    feats = lift_high.shape[0]
    high, low = split(x.reshape(4 * channels, columns))
    at = [slice(k * channels, (k + 3) * channels) for k in range(2)]
    high = jnp.concatenate([high[s] for s in at], axis=1)
    low = jnp.concatenate([low[s] for s in at], axis=1)
    y = mm(conv_high[...], high) + (mm(conv_low[...], high) + mm(conv_high[...], low))
    hidden = []
    for k in range(2):
        h = jnp.maximum(from_columns(y[:, k * columns : (k + 1) * columns], channels), 0.0)
        hidden.append(jnp.where(inside[k], h, 0.0))
    high, low = split(jnp.concatenate(hidden, axis=1))
    f = mm(lift_high[...], high) + (mm(lift_low[...], high) + mm(lift_high[...], low))
    for k in range(2):
        to[k * feats : (k + 1) * feats] = f[:, k * columns : (k + 1) * columns]


def four_rows(half, block, beside):
    a, b = block[...], beside[...]
    first = half == 1
    return jnp.concatenate([jnp.where(first, a, b), jnp.where(first, b, a)], axis=0)


def rows_inside(flags, half):
    return [jnp.logical_or(half != k, flags[2 + k] == 1) for k in range(2)]


def prepare_kernel(flags, conv_hbm, lift_hbm, vol_hbm, own_hbm, mate, conv_high, conv_low, lift_high, lift_low, banded, anchor, conv, lift, vol, own, sems):
    pairs = ((conv_hbm, conv), (lift_hbm, lift), (vol_hbm, vol), (own_hbm, own))
    copies = [pltpu.make_async_copy(a, b, sems.at[i]) for i, (a, b) in enumerate(pairs)]
    for copy in copies:
        copy.start()
    channels = conv.shape[2]
    copies[0].wait()
    for dr in range(3):
        for dc in range(3):
            high, low = split(conv[dr, dc])
            at = (slice(dc * channels, (dc + 1) * channels), slice(dr * channels, (dr + 1) * channels))
            conv_high[at] = high
            conv_low[at] = low
    feats = lift.shape[0]
    per = feats // GROUPS
    copies[1].wait()
    for g in range(0, feats, 8 * per):
        ordered = jnp.concatenate([lift[pl.ds(g + j, 8, stride=per)] for j in range(per)], axis=0)
        high, low = split(ordered)
        lift_high[g : g + 8 * per] = high
        lift_low[g : g + 8 * per] = low
    outs = vol.shape[3]
    m = 3 * outs
    nothing = jnp.zeros((m, GROUPS), F32)
    copies[2].wait()
    for half in range(2):
        for row in range(2):
            pieces = []
            for dd in range(3):
                for place in range(2):
                    dr = 2 * half + place - row
                    pieces.append(vol[dr, dd].reshape(m, GROUPS) * (1.0 / per) if 0 <= dr < 3 else nothing)
            high, low = split(jnp.concatenate(pieces, axis=1))
            banded[(4 * half + row) * m : (4 * half + row + 1) * m] = high
            banded[(4 * half + 2 + row) * m : (4 * half + 3 + row) * m] = low
    half = 1 - flags[1]
    copies[3].wait()
    features(four_rows(half, own, mate), (conv_high, conv_low, lift_high, lift_low), anchor, rows_inside(flags, half))


def correlate(right, anchor, other, shifted, c_high, c_low, per):
    columns = anchor.shape[1]
    column = lax.broadcasted_iota(jnp.int32, (8, columns), 1)
    place = jnp.where(right, columns - 1 - column, column)

    def along(x, d):
        if d == 0:
            return x
        there, back = d % columns, -d % columns
        return pltpu.roll(x, jnp.where(right, back, there), 1)

    slab = 2 * GROUPS
    nothing = jnp.zeros((slab, columns), BF16)
    for c in (c_high, c_low):
        c[:slab] = nothing
        c[(DISP + 1) * slab :] = nothing
    block = 8 * per
    blocks = [slice(i * block, (i + 1) * block) for i in range(slab // 8)]
    for at in blocks:
        values = other[at]
        for b in range(1, STEP):
            shifted[b, at] = along(values, b)
    for a in range(0, DISP, STEP):
        for i in range(0, len(blocks), 2):
            moved = [along(anchor[at], -a) for at in blocks[i : i + 2]]
            for b in range(min(STEP, DISP - a)):
                d = a + b
                tiles = []
                for m, at in zip(moved, blocks[i : i + 2]):
                    c = jnp.sum((m * (shifted[b, at] if b else other[at])).reshape(per, 8, columns), axis=0)
                    c = along(c, a)
                    tiles.append(jnp.where(place >= d, c, 0.0) if d else c)
                high, low = split(jnp.concatenate(tiles, axis=0))
                at = slice((d + 1) * slab + i * 8, (d + 1) * slab + i * 8 + 16)
                c_high[at] = high
                c_low[at] = low


def filtered_pairs(half, banded, c_high, c_low):
    slab = 2 * GROUPS
    m = banded.shape[0] // 4
    weight = banded[pl.ds(pl.multiple_of(half * 2 * m, 2 * m), 2 * m)]
    for d in range(0, DISP, 2):
        at = [slice((d + k) * slab, (d + k + 3) * slab) for k in range(2)]
        high = jnp.concatenate([c_high[s] for s in at], axis=1)
        low = jnp.concatenate([c_low[s] for s in at], axis=1)
        y = mm(weight, high)
        yield d, y[:m] + (y[m:] + mm(weight[:m], low))


def near_kernel(flags, partner, mate, anchor, conv_high, conv_low, lift_high, lift_low, banded, out, other, shifted, c_high, c_low):
    half = 1 - flags[1]
    operands = (conv_high, conv_low, lift_high, lift_low)
    features(four_rows(half, partner, mate), operands, other, rows_inside(flags, half))
    per = lift_high.shape[0] // GROUPS
    correlate(flags[0] == 1, anchor, other, shifted, c_high, c_low, per)
    for d, y in filtered_pairs(half, banded, c_high, c_low):
        out[d // 2] = y


def far_kernel(flags, own, own_far, partner, partner_far, conv_high, conv_low, lift_high, lift_low, banded, part, out, anchor, other, shifted, c_high, c_low):
    half = flags[1]
    operands = (conv_high, conv_low, lift_high, lift_low)
    features(four_rows(half, partner, partner_far), operands, other, rows_inside(flags, half))
    features(four_rows(half, own, own_far), operands, anchor, rows_inside(flags, half))
    per = lift_high.shape[0] // GROUPS
    correlate(flags[0] == 1, anchor, other, shifted, c_high, c_low, per)
    columns = own.shape[2]
    outs = banded.shape[0] // 24
    for d, y in filtered_pairs(half, banded, c_high, c_low):
        y = y + part[d // 2]
        for k in range(2):
            for row in range(2):
                o = from_columns(y[row * 3 * outs : (row + 1) * 3 * outs, k * columns : (k + 1) * columns], outs)
                out[pl.ds(row * outs * DISP + d + k, outs, stride=DISP)] = o


def vmem():
    return pl.BlockSpec(memory_space=pltpu.VMEM)


def smem():
    return pl.BlockSpec(memory_space=pltpu.SMEM)


def call(kernel, name, out_shape, scratch, flags, *args, in_hbm=0):
    return pl.pallas_call(
        kernel,
        out_shape=out_shape,
        in_specs=[smem()] + [pl.BlockSpec(memory_space=pltpu.HBM)] * in_hbm + [vmem()] * (len(args) - in_hbm),
        out_specs=jax.tree.map(lambda _: vmem(), out_shape),
        scratch_shapes=scratch,
        compiler_params=pltpu.CompilerParams(vmem_limit_bytes=VMEM_BYTES),
        cost_estimate=pl.CostEstimate(flops=COST, bytes_accessed=COST, transcendentals=0),
        name=name,
    )(flags, *args)


def prepare(flags, conv, lift, vol, own, mate):
    channels, columns = own.shape[1:]
    feats = lift.shape[0]
    shapes = [(3 * channels, 3 * channels)] * 2 + [(feats, channels)] * 2 + [(8 * 3 * vol.shape[3], 6 * GROUPS)]
    out = [jax.ShapeDtypeStruct(s, BF16) for s in shapes] + [jax.ShapeDtypeStruct((2 * feats, columns), F32)]
    scratch = [pltpu.VMEM(x.shape, F32) for x in (conv, lift, vol, own)] + [pltpu.SemaphoreType.DMA((4,))]
    *operands, anchor = call(prepare_kernel, "prepare", out, scratch, flags, *[pltpu.with_memory_space_constraint(x, pltpu.HBM) for x in (conv, lift, vol, own)], mate, in_hbm=4)
    return operands, anchor


def volume_scratch(feats, columns):
    depth = (DISP + 2) * 2 * GROUPS
    return [pltpu.VMEM((2 * feats, columns), F32), pltpu.VMEM((STEP, 2 * feats, columns), F32)] + [pltpu.VMEM((depth, columns), BF16)] * 2


def near(flags, partner, mate, anchor, operands):
    columns = partner.shape[2]
    feats = operands[2].shape[0]
    out = jax.ShapeDtypeStruct((DISP // 2, operands[4].shape[0] // 4, 2 * columns), F32)
    return call(near_kernel, "near", out, volume_scratch(feats, columns), flags, partner, mate, anchor, *operands)


def far(flags, own, own_far, partner, partner_far, operands, part):
    columns = own.shape[2]
    feats = operands[2].shape[0]
    out = jax.ShapeDtypeStruct((2 * operands[4].shape[0] // 24 * DISP, columns), F32)
    scratch = [pltpu.VMEM((2 * feats, columns), F32)] + volume_scratch(feats, columns)
    return call(far_kernel, "far", out, scratch, flags, own, own_far, partner, partner_far, *operands, part)


def routes(size):
    half, quarter = size // 2, size // 4

    def across(i):
        return (i + 1) % size if i % 2 else (i - 1) % size

    def apart(i, j):
        low, high = min(i, j), max(i, j)
        return high - low == 1 and high in (quarter, 3 * quarter)

    every = range(size)
    swap = [(i, (i + half) % size) for i in every]
    mates = [(i, i ^ 1) for i in every if not apart(i, i ^ 1)]
    far = [(across(i), i) for i in every if not apart(i, across(i))]
    far_partner = [((i + half) % size, j) for i, j in far]
    return swap, mates, far, far_partner


def on_device(images, conv_weight, lift_weight, vol_weight):
    size = lax.axis_size("rows")
    position = lax.axis_index("rows")
    quarter = size // 4
    swap, mates, beyond, beyond_partner = routes(size)
    starts = (position == quarter) | (position == 3 * quarter)
    ends = (position == quarter - 1) | (position == 3 * quarter - 1)
    right = (position < quarter) | (position >= 3 * quarter)
    flags = jnp.stack([jnp.where(right, 1, 0), position % 2, jnp.where(starts, 0, 1), jnp.where(ends, 0, 1)]).astype(jnp.int32)

    partner = lax.ppermute(images, "rows", swap)
    partner_far = lax.ppermute(images, "rows", beyond_partner)
    own_mate = lax.ppermute(images, "rows", mates)
    own_far = lax.ppermute(images, "rows", beyond)
    partner_mate = lax.ppermute(partner, "rows", mates)
    operands, anchor = prepare(flags, conv_weight, lift_weight, vol_weight, images, own_mate)
    part = near(flags, partner, partner_mate, anchor, operands)
    whole = far(flags, images, own_far, partner, partner_far, operands, part)
    rows, _, columns = images.shape
    return whole.reshape(rows, vol_weight.shape[3], DISP, columns)


def solution(mesh):
    return jax.shard_map(
        on_device,
        mesh=mesh,
        in_specs=(P(("scenes", "rows"), None, None), P(), P(), P()),
        out_specs=P(("scenes", "rows"), None, None, None),
        check_vma=False,
    )
```

time: 254 us -> 27.3 us (0.11)
  the two profiles are of different devices: /device:TPU:1 before, /device:TPU:25 now
where the time goes in v2:
time: 27.3 us; the launch traced here: 27.1 us
  Pallas kernels  15.8 us (58%)
  starting transfers between devices  9.18 us (34%)
  waiting for transfers between devices  1.92 us (7%)
    pallas_call x3, Pallas kernels, call(): pl.pallas_call(kernel, out_shape=out_shape, in_specs=[smem()] + [pl.Block...  15.8 us
    ppermute x1, starting transfers between devices, on_device(): partner_far = lax.ppermute(images, 'rows', beyond_partner)  5.05 us
    ppermute x1, starting transfers between devices, on_device(): own_far = lax.ppermute(images, 'rows', beyond)  2.53 us
    ppermute x1, waiting for transfers between devices, on_device(): partner = lax.ppermute(images, 'rows', swap)  1.91 us
    ppermute x1, starting transfers between devices, on_device(): own_mate = lax.ppermute(images, 'rows', mates)  0.96 us
    ppermute x1, starting transfers between devices, on_device(): partner_mate = lax.ppermute(partner, 'rows', mates)  0.59 us
  transfers between devices with their start and end apart: 5, of which 1 were waited for; matrix products, arithmetic and copies ran while one was open for 0% of the time, Pallas kernels for 29%

profile of v2, /device:TPU:25, one launch (start us, length us, event | category | flops | bytes accessed | tf_op | source)
XLA Modules:
  0.0 27.1 jit_solution(10006839117915541661)
XLA Ops:
  0.0 0.1 collective-permute-start.1
  0.1 1.0 %collective-permute-start.3 = (f32[2,128,128]{2,1,0:T(8,128)}, f32[2,128,128]{2,1,0:T(8,128)S(1)}, u32[]{:S(2)}, u32[]{:S(2)}) collective-permute-start(f32[2,128,128]{2,1,0:T(8,128)} %own.1), channel_id=1, source_target_pairs={{0,1},{1,0},{2,3},{3,2},{4,5},{5,4},{6,7},{7,6},{8,9},{9,8},{10,11... | collective-permute-start | bytes 393224 | tf_op jit(solution)/shard_map/ppermute | solution.py:262
  1.0 5.1 %collective-permute-start.2 = (f32[2,128,128]{2,1,0:T(8,128)}, f32[2,128,128]{2,1,0:T(8,128)}, u32[]{:S(2)}, u32[]{:S(2)}) collective-permute-start(f32[2,128,128]{2,1,0:T(8,128)} %own.1), channel_id=1, source_target_pairs={{7,0},{10,1},{9,2},{14,5},{13,6},{0,7},{15,8},{2,9},{1,10},{6,13},... | collective-permute-start | bytes 393224 | tf_op jit(solution)/shard_map/ppermute | solution.py:261
  6.1 2.5 %collective-permute-start = (f32[2,128,128]{2,1,0:T(8,128)}, f32[2,128,128]{2,1,0:T(8,128)}, u32[]{:S(2)}, u32[]{:S(2)}) collective-permute-start(f32[2,128,128]{2,1,0:T(8,128)} %own.1), channel_id=1, source_target_pairs={{15,0},{2,1},{1,2},{6,5},{5,6},{8,7},{7,8},{10,9},{9,10},{14,13},{... | collective-permute-start | bytes 393224 | tf_op jit(solution)/shard_map/ppermute | solution.py:263
  8.6 0.1 pad_add_fusion.flags
  8.7 1.9 %collective-permute-done.1.partner = f32[2,128,128]{2,1,0:T(8,128)S(1)} collective-permute-done((f32[2,128,128]{2,1,0:T(8,128)}, f32[2,128,128]{2,1,0:T(8,128)S(1)}, u32[]{:S(2)}, u32[]{:S(2)}) %collective-permute-start.1) | collective-permute-done | bytes 131104 | tf_op jit(solution)/shard_map/ppermute | solution.py:260
  10.6 0.6 %collective-permute-start.4 = (f32[2,128,128]{2,1,0:T(8,128)S(1)}, f32[2,128,128]{2,1,0:T(8,128)S(1)}, u32[]{:S(2)}, u32[]{:S(2)}) collective-permute-start(f32[2,128,128]{2,1,0:T(8,128)S(1)} %collective-permute-done.1.partner), channel_id=1, source_target_pairs={{0,1},{1,0},{2,3},{3,2},{4,5},{5,4},{6,7},{7,6},{8,9},{9,8},{10,11... | collective-permute-start | bytes 393224 | tf_op jit(solution)/shard_map/ppermute | solution.py:264
  11.2 0.0 collective-permute-done.3.mate
  11.2 3.1 %prepare.1 = (bf16[384,384]{1,0:T(8,128)(2,1)S(1)}, bf16[384,384]{1,0:T(8,128)(2,1)S(1)}, bf16[320,128]{1,0:T(8,128)(2,1)S(1)}, bf16[320,128]{1,0:T(8,128)(2,1)S...) custom-call(s32[4]{0:T(128)S(1)} %pad_add_fusion.flags, f32[3,3,128,128]{3,2,1,0:T(8,128)} %conv_hbm.1, ...), custom_call_target="tpu_custom_call" | custom-call | flops 99999997952 | bytes 99999997952 | tf_op jit(solution)/shard_map/prepare/pallas_call | solution.py:190
  14.3 0.0 collective-permute-done.4.mate
  14.3 0.0 copy-start
  14.4 4.8 %near.1.part = f32[24,192,256]{2,1,0:T(8,128)S(1)} custom-call(s32[4]{0:T(128)S(1)} %pad_add_fusion.flags, f32[2,128,128]{2,1,0:T(8,128)S(1)} %collective-permute-done.1.partner, f32[2,128,128]{2,1,0:T(8,128)S(1)} %collective-permute-done.4.mate, f32[640,128]{1,0:T(8,128)S(1)} %get-tuple-element.16.anchor, bf16[384,384]{1,0:T(8,128)(2,1)S(1)} %get-tuple-element.11.conv_high, ...), custom_call_target="tpu_custom_call" | custom-call | flops 99999997952 | bytes 99999997952 | tf_op jit(solution)/shard_map/near/pallas_call | solution.py:190
  19.1 0.0 collective-permute-done.2.partner_far
  19.1 0.0 collective-permute-done.own_far
  19.1 0.0 copy-done
  19.2 7.9 %far.1 = f32[3072,128]{1,0:T(8,128)} custom-call(s32[4]{0:T(128)S(1)} %pad_add_fusion.flags, f32[2,128,128]{2,1,0:T(8,128)S(1)} %copy-done, f32[2,128,128]{2,1,0:T(8,128)} %collective-permute-done.own_far, f32[2,128,128]{2,1,0:T(8,128)S(1)} %collective-permute-done.1.partner, f32[2,128,128]{2,1,0:T(8,128)} %collective-permute-done.2.partner_far, ...), custom_call_target="tpu_custom_call" | custom-call | flops 99999997952 | bytes 99999997952 | tf_op jit(solution)/shard_map/far/pallas_call | solution.py:190
Async XLA Ops:
  0.0 10.6 %collective-permute-start.1 = (f32[2,128,128]{2,1,0:T(8,128)}, f32[2,128,128]{2,1,0:T(8,128)S(1)}, u32[]{:S(2)}, u32[]{:S(2)}) collective-permute-start(f32[2,128,128]{2,1,0:T(8,128)} %own.1), channel_id=1, source_target_pairs={{0,8},{1,9},{2,10},{3,11},{4,12},{5,13},{6,14},{7,15},{8,0},{9,1},... | collective-permute-start | bytes 393224 | tf_op jit(solution)/shard_map/ppermute | solution.py:260
  0.1 11.2 %collective-permute-start.3 = (f32[2,128,128]{2,1,0:T(8,128)}, f32[2,128,128]{2,1,0:T(8,128)S(1)}, u32[]{:S(2)}, u32[]{:S(2)}) collective-permute-start(f32[2,128,128]{2,1,0:T(8,128)} %own.1), channel_id=1, source_target_pairs={{0,1},{1,0},{2,3},{3,2},{4,5},{5,4},{6,7},{7,6},{8,9},{9,8},{10,11... | collective-permute-start | bytes 393224 | tf_op jit(solution)/shard_map/ppermute | solution.py:262
  1.0 18.1 %collective-permute-start.2 = (f32[2,128,128]{2,1,0:T(8,128)}, f32[2,128,128]{2,1,0:T(8,128)}, u32[]{:S(2)}, u32[]{:S(2)}) collective-permute-start(f32[2,128,128]{2,1,0:T(8,128)} %own.1), channel_id=1, source_target_pairs={{7,0},{10,1},{9,2},{14,5},{13,6},{0,7},{15,8},{2,9},{1,10},{6,13},... | collective-permute-start | bytes 393224 | tf_op jit(solution)/shard_map/ppermute | solution.py:261
  6.1 13.1 %collective-permute-start = (f32[2,128,128]{2,1,0:T(8,128)}, f32[2,128,128]{2,1,0:T(8,128)}, u32[]{:S(2)}, u32[]{:S(2)}) collective-permute-start(f32[2,128,128]{2,1,0:T(8,128)} %own.1), channel_id=1, source_target_pairs={{15,0},{2,1},{1,2},{6,5},{5,6},{8,7},{7,8},{10,9},{9,10},{14,13},{... | collective-permute-start | bytes 393224 | tf_op jit(solution)/shard_map/ppermute | solution.py:263
  10.6 3.7 %collective-permute-start.4 = (f32[2,128,128]{2,1,0:T(8,128)S(1)}, f32[2,128,128]{2,1,0:T(8,128)S(1)}, u32[]{:S(2)}, u32[]{:S(2)}) collective-permute-start(f32[2,128,128]{2,1,0:T(8,128)S(1)} %collective-permute-done.1.partner), channel_id=1, source_target_pairs={{0,1},{1,0},{2,3},{3,2},{4,5},{5,4},{6,7},{7,6},{8,9},{9,8},{10,11... | collective-permute-start | bytes 393224 | tf_op jit(solution)/shard_map/ppermute | solution.py:264
  14.3 4.8 %copy-start = (f32[2,128,128]{2,1,0:T(8,128)S(1)}, f32[2,128,128]{2,1,0:T(8,128)}, u32[]{:S(2)}) copy-start(f32[2,128,128]{2,1,0:T(8,128)} %own.1) | copy-start | bytes 393220

commit v3 on v2

v3 whole, which is shorter than its diff:
```python
import jax
import jax.numpy as jnp
from jax import lax
from jax.experimental import pallas as pl
from jax.experimental.pallas import tpu as pltpu
from jax.sharding import PartitionSpec as P

GROUPS = 40
DISP = 48
STEP = 8
COST = 10**11
F32 = jnp.float32
BF16 = jnp.bfloat16
VMEM_BYTES = 24 * 1024 * 1024


def split(x):
    high = x.astype(BF16)
    return high, (x - high.astype(F32)).astype(BF16)


def mm(a, b):
    return jnp.dot(a, b, preferred_element_type=F32)


def from_columns(y, size):
    column = lax.broadcasted_iota(jnp.int32, (size, y.shape[1]), 1)
    last = y.shape[1] - 1
    left = jnp.where(column > 0, pltpu.roll(y[:size], 1, 1), 0.0)
    right = jnp.where(column < last, pltpu.roll(y[2 * size :], last, 1), 0.0)
    return y[size : 2 * size] + left + right


def features(fours, operands, tos, inside):
    conv_high, conv_low, lift_high, lift_low = operands
    channels = conv_high.shape[0] // 3
    columns = fours[0].shape[2]
    feats = lift_high.shape[0]
    at = [slice(k * channels, (k + 3) * channels) for k in range(2)]
    products = []
    for x in fours:
        high, low = split(x.reshape(4 * channels, columns))
        high = jnp.concatenate([high[s] for s in at], axis=1)
        low = jnp.concatenate([low[s] for s in at], axis=1)
        products.append(mm(conv_high[...], high) + (mm(conv_low[...], high) + mm(conv_high[...], low)))
    halves = []
    for y in products:
        hidden = []
        for k in range(2):
            h = jnp.maximum(from_columns(y[:, k * columns : (k + 1) * columns], channels), 0.0)
            hidden.append(jnp.where(inside[k], h, 0.0))
        halves.append(split(jnp.concatenate(hidden, axis=1)))
    for (high, low), to in zip(halves, tos):
        f = mm(lift_high[...], high) + (mm(lift_low[...], high) + mm(lift_high[...], low))
        for k in range(2):
            to[k * feats : (k + 1) * feats] = f[:, k * columns : (k + 1) * columns]


def four_rows(half, block, beside):
    a, b = block[...], beside[...]
    first = half == 1
    return jnp.concatenate([jnp.where(first, a, b), jnp.where(first, b, a)], axis=0)


def rows_inside(flags, half):
    return [jnp.logical_or(half != k, flags[2 + k] == 1) for k in range(2)]


def prepare_kernel(conv_hbm, lift_hbm, vol_hbm, conv_high, conv_low, lift_high, lift_low, banded, conv, lift, vol, sems):
    pairs = ((conv_hbm, conv), (lift_hbm, lift), (vol_hbm, vol))
    copies = [pltpu.make_async_copy(a, b, sems.at[i]) for i, (a, b) in enumerate(pairs)]
    for copy in copies:
        copy.start()
    channels = conv.shape[2]
    copies[0].wait()
    for dr in range(3):
        for dc in range(3):
            high, low = split(conv[dr, dc])
            at = (slice(dc * channels, (dc + 1) * channels), slice(dr * channels, (dr + 1) * channels))
            conv_high[at] = high
            conv_low[at] = low
    feats = lift.shape[0]
    per = feats // GROUPS
    copies[1].wait()
    for g in range(0, feats, 8 * per):
        ordered = jnp.concatenate([lift[pl.ds(g + j, 8, stride=per)] for j in range(per)], axis=0)
        high, low = split(ordered)
        lift_high[g : g + 8 * per] = high
        lift_low[g : g + 8 * per] = low
    outs = vol.shape[3]
    m = 3 * outs
    nothing = jnp.zeros((m, GROUPS), F32)
    copies[2].wait()
    for half in range(2):
        for row in range(2):
            pieces = []
            for dd in range(3):
                for place in range(2):
                    dr = 2 * half + place - row
                    pieces.append(vol[dr, dd].reshape(m, GROUPS) * (1.0 / per) if 0 <= dr < 3 else nothing)
            high, low = split(jnp.concatenate(pieces, axis=1))
            banded[(4 * half + row) * m : (4 * half + row + 1) * m] = high
            banded[(4 * half + 2 + row) * m : (4 * half + 3 + row) * m] = low


def mover(right, columns):
    def along(x, d):
        if d == 0:
            return x
        there, back = d % columns, -d % columns
        return pltpu.roll(x, jnp.where(right, back, there), 1)

    return along


def blocks_of(per):
    block = 8 * per
    return [slice(i * block, (i + 1) * block) for i in range(2 * GROUPS // 8)]


def move_other(right, other, shifted, per):
    along = mover(right, other.shape[1])
    for at in blocks_of(per):
        values = other[at]
        for b in range(1, STEP):
            shifted[b - 1, at] = along(values, b)


def move_anchor(right, anchor, moved, per):
    along = mover(right, anchor.shape[1])
    for k, a in enumerate(range(STEP, DISP, STEP)):
        for at in blocks_of(per):
            moved[k, at] = along(anchor[at], -a)


def correlate(right, anchor, moved, other, shifted, c_high, c_low, per):
    columns = anchor.shape[1]
    along = mover(right, columns)
    column = lax.broadcasted_iota(jnp.int32, (8, columns), 1)
    place = jnp.where(right, columns - 1 - column, column)
    slab = 2 * GROUPS
    nothing = jnp.zeros((slab, columns), BF16)
    for c in (c_high, c_low):
        c[:slab] = nothing
        c[(DISP + 1) * slab :] = nothing
    blocks = blocks_of(per)
    for k, a in enumerate(range(0, DISP, STEP)):
        for i in range(0, len(blocks), 2):
            ours = [moved[k - 1, at] if k else anchor[at] for at in blocks[i : i + 2]]
            for b in range(min(STEP, DISP - a)):
                d = a + b
                tiles = []
                for m, at in zip(ours, blocks[i : i + 2]):
                    c = jnp.sum((m * (shifted[b - 1, at] if b else other[at])).reshape(per, 8, columns), axis=0)
                    c = along(c, a)
                    tiles.append(jnp.where(place >= d, c, 0.0) if d else c)
                high, low = split(jnp.concatenate(tiles, axis=0))
                at = slice((d + 1) * slab + i * 8, (d + 1) * slab + i * 8 + 16)
                c_high[at] = high
                c_low[at] = low


def filtered_pairs(half, banded, c_high, c_low):
    slab = 2 * GROUPS
    m = banded.shape[0] // 4
    weight = banded[pl.ds(pl.multiple_of(half * 2 * m, 2 * m), 2 * m)]
    for d in range(0, DISP, 2):
        at = [slice((d + k) * slab, (d + k + 3) * slab) for k in range(2)]
        high = jnp.concatenate([c_high[s] for s in at], axis=1)
        low = jnp.concatenate([c_low[s] for s in at], axis=1)
        y = mm(weight, high)
        yield d, y[:m] + (y[m:] + mm(weight[:m], low))


def near_kernel(flags, own, own_mate, partner, partner_mate, partner_far, conv_high, conv_low, lift_high, lift_low, banded, part, far_other, anchor, other, moved, shifted, c_high, c_low):
    half = 1 - flags[1]
    right = flags[0] == 1
    operands = (conv_high, conv_low, lift_high, lift_low)
    per = lift_high.shape[0] // GROUPS
    fours = [four_rows(half, own, own_mate), four_rows(half, partner, partner_mate)]
    features(fours, operands, [anchor, other], rows_inside(flags, half))
    move_anchor(right, anchor, moved, per)
    move_other(right, other, shifted, per)
    features([four_rows(1 - half, partner, partner_far)], operands, [far_other], rows_inside(flags, 1 - half))
    correlate(right, anchor, moved, other, shifted, c_high, c_low, per)
    for d, y in filtered_pairs(half, banded, c_high, c_low):
        part[d // 2] = y


def far_kernel(flags, own, own_far, other, conv_high, conv_low, lift_high, lift_low, banded, part, out, anchor, moved, shifted, c_high, c_low):
    half = flags[1]
    right = flags[0] == 1
    operands = (conv_high, conv_low, lift_high, lift_low)
    per = lift_high.shape[0] // GROUPS
    move_other(right, other, shifted, per)
    features([four_rows(half, own, own_far)], operands, [anchor], rows_inside(flags, half))
    move_anchor(right, anchor, moved, per)
    correlate(right, anchor, moved, other, shifted, c_high, c_low, per)
    columns = own.shape[2]
    outs = banded.shape[0] // 24
    for d, y in filtered_pairs(half, banded, c_high, c_low):
        y = y + part[d // 2]
        for k in range(2):
            for row in range(2):
                o = from_columns(y[row * 3 * outs : (row + 1) * 3 * outs, k * columns : (k + 1) * columns], outs)
                out[pl.ds(row * outs * DISP + d + k, outs, stride=DISP)] = o


def vmem():
    return pl.BlockSpec(memory_space=pltpu.VMEM)


def smem():
    return pl.BlockSpec(memory_space=pltpu.SMEM)


def call(kernel, name, out_shape, in_specs, scratch, *args):
    return pl.pallas_call(
        kernel,
        out_shape=out_shape,
        in_specs=in_specs,
        out_specs=jax.tree.map(lambda _: vmem(), out_shape),
        scratch_shapes=scratch,
        compiler_params=pltpu.CompilerParams(vmem_limit_bytes=VMEM_BYTES),
        cost_estimate=pl.CostEstimate(flops=COST, bytes_accessed=COST, transcendentals=0),
        name=name,
    )(*args)


def prepare(conv, lift, vol):
    channels = conv.shape[2]
    feats = lift.shape[0]
    shapes = [(3 * channels, 3 * channels)] * 2 + [(feats, channels)] * 2 + [(8 * 3 * vol.shape[3], 6 * GROUPS)]
    out = [jax.ShapeDtypeStruct(s, BF16) for s in shapes]
    scratch = [pltpu.VMEM(x.shape, F32) for x in (conv, lift, vol)] + [pltpu.SemaphoreType.DMA((3,))]
    args = [pltpu.with_memory_space_constraint(x, pltpu.HBM) for x in (conv, lift, vol)]
    return call(prepare_kernel, "prepare", out, [pl.BlockSpec(memory_space=pltpu.HBM)] * 3, scratch, *args)


def volume_scratch(feats, columns):
    depth = (DISP + 2) * 2 * GROUPS
    return [
        pltpu.VMEM((-(-DISP // STEP) - 1, 2 * feats, columns), F32),
        pltpu.VMEM((STEP - 1, 2 * feats, columns), F32),
        pltpu.VMEM((depth, columns), BF16),
        pltpu.VMEM((depth, columns), BF16),
    ]


def near(flags, own, own_mate, partner, partner_mate, partner_far, operands):
    columns = partner.shape[2]
    feats = operands[2].shape[0]
    out = [
        jax.ShapeDtypeStruct((DISP // 2, operands[4].shape[0] // 4, 2 * columns), F32),
        jax.ShapeDtypeStruct((2 * feats, columns), F32),
    ]
    scratch = [pltpu.VMEM((2 * feats, columns), F32)] * 2 + volume_scratch(feats, columns)
    args = (own, own_mate, partner, partner_mate, partner_far, *operands)
    return call(near_kernel, "near", out, [smem()] + [vmem()] * len(args), scratch, flags, *args)


def far(flags, own, own_far, other, operands, part):
    columns = own.shape[2]
    feats = operands[2].shape[0]
    out = jax.ShapeDtypeStruct((2 * operands[4].shape[0] // 24 * DISP, columns), F32)
    scratch = [pltpu.VMEM((2 * feats, columns), F32)] + volume_scratch(feats, columns)
    args = (own, own_far, other, *operands, part)
    return call(far_kernel, "far", out, [smem()] + [vmem()] * len(args), scratch, flags, *args)


def routes(size):
    half, quarter = size // 2, size // 4

    def across(i):
        return (i + 1) % size if i % 2 else (i - 1) % size

    def apart(i, j):
        low, high = min(i, j), max(i, j)
        return high - low == 1 and high in (quarter, 3 * quarter)

    every = range(size)
    swap = [(i, (i + half) % size) for i in every]
    mates = [(i, i ^ 1) for i in every if not apart(i, i ^ 1)]
    far = [(across(i), i) for i in every if not apart(i, across(i))]
    far_partner = [((i + half) % size, j) for i, j in far]
    return swap, mates, far, far_partner


def on_device(images, conv_weight, lift_weight, vol_weight):
    size = lax.axis_size("rows")
    position = lax.axis_index("rows")
    quarter = size // 4
    swap, mates, beyond, beyond_partner = routes(size)
    starts = (position == quarter) | (position == 3 * quarter)
    ends = (position == quarter - 1) | (position == 3 * quarter - 1)
    right = (position < quarter) | (position >= 3 * quarter)
    flags = jnp.stack([jnp.where(right, 1, 0), position % 2, jnp.where(starts, 0, 1), jnp.where(ends, 0, 1)]).astype(jnp.int32)

    partner = lax.ppermute(images, "rows", swap)
    partner_far = lax.ppermute(images, "rows", beyond_partner)
    own_mate = lax.ppermute(images, "rows", mates)
    own_far = lax.ppermute(images, "rows", beyond)
    partner_mate = lax.ppermute(partner, "rows", mates)
    operands = prepare(conv_weight, lift_weight, vol_weight)
    part, other = near(flags, images, own_mate, partner, partner_mate, partner_far, operands)
    whole = far(flags, images, own_far, other, operands, part)
    rows, _, columns = images.shape
    return whole.reshape(rows, vol_weight.shape[3], DISP, columns)


def solution(mesh):
    return jax.shard_map(
        on_device,
        mesh=mesh,
        in_specs=(P(("scenes", "rows"), None, None), P(), P(), P()),
        out_specs=P(("scenes", "rows"), None, None, None),
        check_vma=False,
    )
```

time: 27.3 us -> 25.3 us (0.927)
  the two profiles are of different devices: /device:TPU:25 before, /device:TPU:0 now
where the time goes in v3:
time: 25.3 us; the launch traced here: 25 us
  Pallas kernels  12.7 us (50%)
  starting transfers between devices  12.1 us (48%)
    pallas_call x3, Pallas kernels, call(): pl.pallas_call(kernel, out_shape=out_shape, in_specs=in_specs, out_specs=...  12.7 us
    ppermute x1, starting transfers between devices, on_device(): own_far = lax.ppermute(images, 'rows', beyond)  4.3 us
    ppermute x1, starting transfers between devices, on_device(): partner = lax.ppermute(images, 'rows', swap)  4.04 us
    ppermute x1, starting transfers between devices, on_device(): partner_far = lax.ppermute(images, 'rows', beyond_partner)  3.59 us
  transfers between devices with their start and end apart: 5, of which 0 were waited for; matrix products, arithmetic and copies ran while one was open for 0% of the time, Pallas kernels for 27%

profile of v3, /device:TPU:0, one launch (start us, length us, event | category | flops | bytes accessed | tf_op | source)
XLA Modules:
  0.0 25.0 jit_solution(13474478768992558324)
XLA Ops:
  0.0 0.0 copy-start
  0.0 4.0 %collective-permute-start.2 = (f32[2,128,128]{2,1,0:T(8,128)}, f32[2,128,128]{2,1,0:T(8,128)S(1)}, u32[]{:S(2)}, u32[]{:S(2)}) collective-permute-start(f32[2,128,128]{2,1,0:T(8,128)} %own.3), channel_id=1, source_target_pairs={{0,8},{1,9},{2,10},{3,11},{4,12},{5,13},{6,14},{7,15},{8,0},{9,1},... | collective-permute-start | bytes 393224 | tf_op jit(solution)/shard_map/ppermute | solution.py:299
  4.0 3.6 %collective-permute-start.4 = (f32[2,128,128]{2,1,0:T(8,128)}, f32[2,128,128]{2,1,0:T(8,128)S(1)}, u32[]{:S(2)}, u32[]{:S(2)}) collective-permute-start(f32[2,128,128]{2,1,0:T(8,128)} %own.3), channel_id=1, source_target_pairs={{7,0},{10,1},{9,2},{14,5},{13,6},{0,7},{15,8},{2,9},{1,10},{6,13},... | collective-permute-start | bytes 393224 | tf_op jit(solution)/shard_map/ppermute | solution.py:300
  7.6 0.1 collective-permute-start.1
  7.7 4.3 %collective-permute-start = (f32[2,128,128]{2,1,0:T(8,128)}, f32[2,128,128]{2,1,0:T(8,128)}, u32[]{:S(2)}, u32[]{:S(2)}) collective-permute-start(f32[2,128,128]{2,1,0:T(8,128)} %own.3), channel_id=1, source_target_pairs={{15,0},{2,1},{1,2},{6,5},{5,6},{8,7},{7,8},{10,9},{9,10},{14,13},{... | collective-permute-start | bytes 393224 | tf_op jit(solution)/shard_map/ppermute | solution.py:302
  12.0 0.0 collective-permute-done.2.partner
  12.0 0.1 collective-permute-start.3
  12.1 1.5 %prepare.1 = (bf16[384,384]{1,0:T(8,128)(2,1)S(1)}, bf16[384,384]{1,0:T(8,128)(2,1)S(1)}, bf16[320,128]{1,0:T(8,128)(2,1)S(1)}, bf16[320,128]{1,0:T(8,128)(2,1)S(1)}, bf16[768,240]{1,0:T(8,128)(2,1)S(1)}) custom-call(f32[3,3,128,128]{3,2,1,0:T(8,128)} %conv_hbm.1, f32[320,128]{1,0:T(8,128)} %lift_hbm.1, f32[3,3,3,32,40]{4,3,2,1,0:T(8,128)} %vol_hbm.1), custom_call_target="tpu_custom_call" | custom-call | flops 99999997952 | bytes 99999997952 | tf_op jit(solution)/shard_map/prepare/pallas_call | solution.py:218
  13.7 0.1 pad_add_fusion.flags
  13.8 0.0 collective-permute-done.4.partner_far
  13.8 0.0 collective-permute-done.1.own_mate
  13.8 0.0 collective-permute-done.3.partner_mate
  13.8 0.0 copy-done
  13.8 5.1 %near.1 = (f32[24,192,256]{2,1,0:T(8,128)S(1)}, f32[640,128]{1,0:T(8,128)S(1)}) custom-call(s32[4]{0:T(128)S(1)} %pad_add_fusion.flags, f32[2,128,128]{2,1,0:T(8,128)S(1)} %copy-done, f32[2,128,128]{2,1,0:T(8,128)S(1)} %collective-permute-done.1.own_mate, f32[2,128,128]{2,1,0:T(8,128)S(1)} %collective-permute-done.2.partner, ...), custom_call_target="tpu_custom_call" | custom-call | flops 99999997952 | bytes 99999997952 | tf_op jit(solution)/shard_map/near/pallas_call | solution.py:218
  18.9 0.0 collective-permute-done.own_far
  18.9 6.1 %far.1 = f32[3072,128]{1,0:T(8,128)} custom-call(s32[4]{0:T(128)S(1)} %pad_add_fusion.flags, f32[2,128,128]{2,1,0:T(8,128)S(1)} %copy-done, f32[2,128,128]{2,1,0:T(8,128)} %collective-permute-done.own_far, f32[640,128]{1,0:T(8,128)S(1)} %get-tuple-element.17.other, bf16[384,384]{1,0:T(8,128)(2,1)S(1)} %get-tuple-element.12.conv_high, ...), custom_call_target="tpu_custom_call" | custom-call | flops 99999997952 | bytes 99999997952 | tf_op jit(solution)/shard_map/far/pallas_call | solution.py:218
Async XLA Ops:
  0.0 13.8 %copy-start = (f32[2,128,128]{2,1,0:T(8,128)S(1)}, f32[2,128,128]{2,1,0:T(8,128)}, u32[]{:S(2)}) copy-start(f32[2,128,128]{2,1,0:T(8,128)} %own.3) | copy-start | bytes 393220
  0.0 12.0 %collective-permute-start.2 = (f32[2,128,128]{2,1,0:T(8,128)}, f32[2,128,128]{2,1,0:T(8,128)S(1)}, u32[]{:S(2)}, u32[]{:S(2)}) collective-permute-start(f32[2,128,128]{2,1,0:T(8,128)} %own.3), channel_id=1, source_target_pairs={{0,8},{1,9},{2,10},{3,11},{4,12},{5,13},{6,14},{7,15},{8,0},{9,1},... | collective-permute-start | bytes 393224 | tf_op jit(solution)/shard_map/ppermute | solution.py:299
  4.0 9.7 %collective-permute-start.4 = (f32[2,128,128]{2,1,0:T(8,128)}, f32[2,128,128]{2,1,0:T(8,128)S(1)}, u32[]{:S(2)}, u32[]{:S(2)}) collective-permute-start(f32[2,128,128]{2,1,0:T(8,128)} %own.3), channel_id=1, source_target_pairs={{7,0},{10,1},{9,2},{14,5},{13,6},{0,7},{15,8},{2,9},{1,10},{6,13},... | collective-permute-start | bytes 393224 | tf_op jit(solution)/shard_map/ppermute | solution.py:300
  7.6 6.1 %collective-permute-start.1 = (f32[2,128,128]{2,1,0:T(8,128)}, f32[2,128,128]{2,1,0:T(8,128)S(1)}, u32[]{:S(2)}, u32[]{:S(2)}) collective-permute-start(f32[2,128,128]{2,1,0:T(8,128)} %own.3), channel_id=1, source_target_pairs={{0,1},{1,0},{2,3},{3,2},{4,5},{5,4},{6,7},{7,6},{8,9},{9,8},{10,11... | collective-permute-start | bytes 393224 | tf_op jit(solution)/shard_map/ppermute | solution.py:301
  7.7 11.2 %collective-permute-start = (f32[2,128,128]{2,1,0:T(8,128)}, f32[2,128,128]{2,1,0:T(8,128)}, u32[]{:S(2)}, u32[]{:S(2)}) collective-permute-start(f32[2,128,128]{2,1,0:T(8,128)} %own.3), channel_id=1, source_target_pairs={{15,0},{2,1},{1,2},{6,5},{5,6},{8,7},{7,8},{10,9},{9,10},{14,13},{... | collective-permute-start | bytes 393224 | tf_op jit(solution)/shard_map/ppermute | solution.py:302
  12.0 1.7 %collective-permute-start.3 = (f32[2,128,128]{2,1,0:T(8,128)S(1)}, f32[2,128,128]{2,1,0:T(8,128)S(1)}, u32[]{:S(2)}, u32[]{:S(2)}) collective-permute-start(f32[2,128,128]{2,1,0:T(8,128)S(1)} %collective-permute-done.2.partner), channel_id=1, source_target_pairs={{0,1},{1,0},{2,3},{3,2},{4,5},{5,4},{6,7},{7,6},{8,9},{9,8},{10,11... | collective-permute-start | bytes 393224 | tf_op jit(solution)/shard_map/ppermute | solution.py:303

commit v4 on v3

--- a/solution.py
+++ b/solution.py
@@ -8,6 +8,7 @@
 GROUPS = 40
 DISP = 48
 STEP = 8
+CHUNK = 24
 COST = 10**11
 F32 = jnp.float32
 BF16 = jnp.bfloat16
@@ -31,27 +32,28 @@
     return y[size : 2 * size] + left + right
 
 
-def features(fours, operands, tos, inside):
-    conv_high, conv_low, lift_high, lift_low = operands
-    channels = conv_high.shape[0] // 3
+def stacked(high, low):
+    return jnp.concatenate([high, high, low], axis=0)
+
+
+def features(fours, conv, lift, tos, insides):
+    channels = conv.shape[0] // 3
     columns = fours[0].shape[2]
-    feats = lift_high.shape[0]
+    feats = lift.shape[0]
     at = [slice(k * channels, (k + 3) * channels) for k in range(2)]
     products = []
     for x in fours:
-        high, low = split(x.reshape(4 * channels, columns))
-        high = jnp.concatenate([high[s] for s in at], axis=1)
-        low = jnp.concatenate([low[s] for s in at], axis=1)
-        products.append(mm(conv_high[...], high) + (mm(conv_low[...], high) + mm(conv_high[...], low)))
+        parts = split(x.reshape(4 * channels, columns))
+        products.append(mm(conv[...], stacked(*[jnp.concatenate([part[s] for s in at], axis=1) for part in parts])))
     halves = []
-    for y in products:
+    for y, inside in zip(products, insides):
         hidden = []
         for k in range(2):
             h = jnp.maximum(from_columns(y[:, k * columns : (k + 1) * columns], channels), 0.0)
             hidden.append(jnp.where(inside[k], h, 0.0))
-        halves.append(split(jnp.concatenate(hidden, axis=1)))
-    for (high, low), to in zip(halves, tos):
-        f = mm(lift_high[...], high) + (mm(lift_low[...], high) + mm(lift_high[...], low))
+        halves.append(stacked(*split(jnp.concatenate(hidden, axis=1))))
+    for h, to in zip(halves, tos):
+        f = mm(lift[...], h)
         for k in range(2):
             to[k * feats : (k + 1) * feats] = f[:, k * columns : (k + 1) * columns]
 
@@ -66,27 +68,27 @@
     return [jnp.logical_or(half != k, flags[2 + k] == 1) for k in range(2)]
 
 
-def prepare_kernel(conv_hbm, lift_hbm, vol_hbm, conv_high, conv_low, lift_high, lift_low, banded, conv, lift, vol, sems):
+def prepare_kernel(conv_hbm, lift_hbm, vol_hbm, conv_out, lift_out, banded, conv, lift, vol, sems):
     pairs = ((conv_hbm, conv), (lift_hbm, lift), (vol_hbm, vol))
     copies = [pltpu.make_async_copy(a, b, sems.at[i]) for i, (a, b) in enumerate(pairs)]
     for copy in copies:
         copy.start()
     channels = conv.shape[2]
+    depth = 3 * channels
     copies[0].wait()
     for dr in range(3):
         for dc in range(3):
             high, low = split(conv[dr, dc])
-            at = (slice(dc * channels, (dc + 1) * channels), slice(dr * channels, (dr + 1) * channels))
-            conv_high[at] = high
-            conv_low[at] = low
+            for k, part in enumerate((high, low, high)):
+                at = k * depth + dr * channels
+                conv_out[dc * channels : (dc + 1) * channels, at : at + channels] = part
     feats = lift.shape[0]
     per = feats // GROUPS
     copies[1].wait()
     for g in range(0, feats, 8 * per):
         ordered = jnp.concatenate([lift[pl.ds(g + j, 8, stride=per)] for j in range(per)], axis=0)
         high, low = split(ordered)
-        lift_high[g : g + 8 * per] = high
-        lift_low[g : g + 8 * per] = low
+        lift_out[g : g + 8 * per] = jnp.concatenate([high, low, high], axis=1)
     outs = vol.shape[3]
     m = 3 * outs
     nothing = jnp.zeros((m, GROUPS), F32)
@@ -172,38 +174,45 @@
         yield d, y[:m] + (y[m:] + mm(weight[:m], low))
 
 
-def near_kernel(flags, own, own_mate, partner, partner_mate, partner_far, conv_high, conv_low, lift_high, lift_low, banded, part, far_other, anchor, other, moved, shifted, c_high, c_low):
+def near_kernel(flags, own, own_mate, partner, partner_mate, partner_far, conv, lift, banded, part, far_other, anchor, other, moved, shifted, c_high, c_low):
     half = 1 - flags[1]
     right = flags[0] == 1
-    operands = (conv_high, conv_low, lift_high, lift_low)
-    per = lift_high.shape[0] // GROUPS
-    fours = [four_rows(half, own, own_mate), four_rows(half, partner, partner_mate)]
-    features(fours, operands, [anchor, other], rows_inside(flags, half))
+    per = lift.shape[0] // GROUPS
+    fours = [four_rows(half, own, own_mate), four_rows(half, partner, partner_mate), four_rows(1 - half, partner, partner_far)]
+    insides = [rows_inside(flags, half)] * 2 + [rows_inside(flags, 1 - half)]
+    features(fours, conv, lift, [anchor, other, far_other], insides)
     move_anchor(right, anchor, moved, per)
     move_other(right, other, shifted, per)
-    features([four_rows(1 - half, partner, partner_far)], operands, [far_other], rows_inside(flags, 1 - half))
     correlate(right, anchor, moved, other, shifted, c_high, c_low, per)
     for d, y in filtered_pairs(half, banded, c_high, c_low):
         part[d // 2] = y
 
 
-def far_kernel(flags, own, own_far, other, conv_high, conv_low, lift_high, lift_low, banded, part, out, anchor, moved, shifted, c_high, c_low):
+def far_kernel(flags, own, own_far, other, conv, lift, banded, part, result, anchor, moved, shifted, c_high, c_low, out, sems):
     half = flags[1]
     right = flags[0] == 1
-    operands = (conv_high, conv_low, lift_high, lift_low)
-    per = lift_high.shape[0] // GROUPS
+    per = lift.shape[0] // GROUPS
     move_other(right, other, shifted, per)
-    features([four_rows(half, own, own_far)], operands, [anchor], rows_inside(flags, half))
+    features([four_rows(half, own, own_far)], conv, lift, [anchor], [rows_inside(flags, half)])
     move_anchor(right, anchor, moved, per)
     correlate(right, anchor, moved, other, shifted, c_high, c_low, per)
     columns = own.shape[2]
     outs = banded.shape[0] // 24
+    rows = 2 * outs
+    copies = []
     for d, y in filtered_pairs(half, banded, c_high, c_low):
         y = y + part[d // 2]
         for k in range(2):
             for row in range(2):
                 o = from_columns(y[row * 3 * outs : (row + 1) * 3 * outs, k * columns : (k + 1) * columns], outs)
                 out[pl.ds(row * outs * DISP + d + k, outs, stride=DISP)] = o
+        if (d + 2) % CHUNK == 0:
+            i = d // CHUNK
+            at = (slice(None), pl.ds(i * CHUNK, CHUNK))
+            copies.append(pltpu.make_async_copy(out.reshape(rows, DISP, columns).at[at], result.at[at], sems.at[1 + i]))
+            copies[-1].start()
+    for copy in copies:
+        copy.wait()
 
 
 def vmem():
@@ -214,12 +223,16 @@
     return pl.BlockSpec(memory_space=pltpu.SMEM)
 
 
-def call(kernel, name, out_shape, in_specs, scratch, *args):
+def hbm():
+    return pl.BlockSpec(memory_space=pltpu.HBM)
+
+
+def call(kernel, name, out_shape, in_specs, scratch, *args, out_specs=None):
     return pl.pallas_call(
         kernel,
         out_shape=out_shape,
         in_specs=in_specs,
-        out_specs=jax.tree.map(lambda _: vmem(), out_shape),
+        out_specs=jax.tree.map(lambda _: vmem(), out_shape) if out_specs is None else out_specs,
         scratch_shapes=scratch,
         compiler_params=pltpu.CompilerParams(vmem_limit_bytes=VMEM_BYTES),
         cost_estimate=pl.CostEstimate(flops=COST, bytes_accessed=COST, transcendentals=0),
@@ -230,42 +243,41 @@
 def prepare(conv, lift, vol):
     channels = conv.shape[2]
     feats = lift.shape[0]
-    shapes = [(3 * channels, 3 * channels)] * 2 + [(feats, channels)] * 2 + [(8 * 3 * vol.shape[3], 6 * GROUPS)]
+    shapes = [(3 * channels, 9 * channels), (feats, 3 * channels), (8 * 3 * vol.shape[3], 6 * GROUPS)]
     out = [jax.ShapeDtypeStruct(s, BF16) for s in shapes]
     scratch = [pltpu.VMEM(x.shape, F32) for x in (conv, lift, vol)] + [pltpu.SemaphoreType.DMA((3,))]
     args = [pltpu.with_memory_space_constraint(x, pltpu.HBM) for x in (conv, lift, vol)]
-    return call(prepare_kernel, "prepare", out, [pl.BlockSpec(memory_space=pltpu.HBM)] * 3, scratch, *args)
-
-
-def volume_scratch(feats, columns):
-    depth = (DISP + 2) * 2 * GROUPS
-    return [
-        pltpu.VMEM((-(-DISP // STEP) - 1, 2 * feats, columns), F32),
-        pltpu.VMEM((STEP - 1, 2 * feats, columns), F32),
-        pltpu.VMEM((depth, columns), BF16),
-        pltpu.VMEM((depth, columns), BF16),
-    ]
+    return call(prepare_kernel, "prepare", out, [hbm()] * 3, scratch, *args)
+
+
+def sizes(operands, columns):
+    feats = operands[1].shape[0]
+    plain = (2 * feats, columns)
+    moved = (-(-DISP // STEP) - 1, 2 * feats, columns)
+    shifted = (STEP - 1, 2 * feats, columns)
+    volume = ((DISP + 2) * 2 * GROUPS, columns)
+    part = (DISP // 2, operands[2].shape[0] // 4, 2 * columns)
+    return plain, moved, shifted, volume, part
 
 
 def near(flags, own, own_mate, partner, partner_mate, partner_far, operands):
-    columns = partner.shape[2]
-    feats = operands[2].shape[0]
-    out = [
-        jax.ShapeDtypeStruct((DISP // 2, operands[4].shape[0] // 4, 2 * columns), F32),
-        jax.ShapeDtypeStruct((2 * feats, columns), F32),
-    ]
-    scratch = [pltpu.VMEM((2 * feats, columns), F32)] * 2 + volume_scratch(feats, columns)
+    plain, moved, shifted, volume, part = sizes(operands, own.shape[2])
+    scratch = [pltpu.VMEM(s, F32) for s in (plain, plain, moved, shifted)] + [pltpu.VMEM(volume, BF16)] * 2
     args = (own, own_mate, partner, partner_mate, partner_far, *operands)
+    out = [jax.ShapeDtypeStruct(s, F32) for s in (part, plain)]
     return call(near_kernel, "near", out, [smem()] + [vmem()] * len(args), scratch, flags, *args)
 
 
 def far(flags, own, own_far, other, operands, part):
     columns = own.shape[2]
-    feats = operands[2].shape[0]
-    out = jax.ShapeDtypeStruct((2 * operands[4].shape[0] // 24 * DISP, columns), F32)
-    scratch = [pltpu.VMEM((2 * feats, columns), F32)] + volume_scratch(feats, columns)
+    plain, moved, shifted, volume, _ = sizes(operands, columns)
+    rows = operands[2].shape[0] // 12
+    scratch = [pltpu.VMEM(s, F32) for s in (plain, moved, shifted)] + [pltpu.VMEM(volume, BF16)] * 2
+    scratch += [pltpu.VMEM((rows * DISP, columns), F32), pltpu.SemaphoreType.DMA((1 + DISP // CHUNK,))]
     args = (own, own_far, other, *operands, part)
-    return call(far_kernel, "far", out, [smem()] + [vmem()] * len(args), scratch, flags, *args)
+    in_specs = [smem()] + [vmem()] * len(args)
+    out = jax.ShapeDtypeStruct((rows, DISP, columns), F32)
+    return call(far_kernel, "far", out, in_specs, scratch, flags, *args, out_specs=hbm())
 
 
 def routes(size):

time: 25.3 us -> 24.4 us (0.964)
  Pallas kernels: 12.7 us -> 11.8 us
    pallas_call x3, Pallas kernels: 12.7 us -> 11.8 us  [call(): pl.pallas_call(kernel, out_shape=out_shape, in_specs=in_specs, out_specs=...]
  transfers between devices with their start and end apart: 5 -> 5, of which waited for: 0 -> 0; matrix products, arithmetic and copies ran while one was open for 0% -> 0% of each run, Pallas kernels for 27% -> 25%
where the time goes in v4:
time: 24.4 us; the launch traced here: 24.1 us
  starting transfers between devices  12.1 us (50%)
  Pallas kernels  11.8 us (48%)
    pallas_call x3, Pallas kernels, call(): pl.pallas_call(kernel, out_shape=out_shape, in_specs=in_specs, out_specs=...  11.8 us
    ppermute x1, starting transfers between devices, on_device(): own_far = lax.ppermute(images, 'rows', beyond)  4.3 us
    ppermute x1, starting transfers between devices, on_device(): partner = lax.ppermute(images, 'rows', swap)  4.04 us
    ppermute x1, starting transfers between devices, on_device(): partner_far = lax.ppermute(images, 'rows', beyond_partner)  3.59 us
  transfers between devices with their start and end apart: 5, of which 0 were waited for; matrix products, arithmetic and copies ran while one was open for 0% of the time, Pallas kernels for 25%

profile of v4, /device:TPU:0, one launch (start us, length us, event | category | flops | bytes accessed | tf_op | source)
XLA Modules:
  0.0 24.1 jit_solution(17627355992090722755)
XLA Ops:
  0.0 0.0 copy-start
  0.0 4.0 %collective-permute-start.2 = (f32[2,128,128]{2,1,0:T(8,128)}, f32[2,128,128]{2,1,0:T(8,128)S(1)}, u32[]{:S(2)}, u32[]{:S(2)}) collective-permute-start(f32[2,128,128]{2,1,0:T(8,128)} %own.3), channel_id=1, source_target_pairs={{0,8},{1,9},{2,10},{3,11},{4,12},{5,13},{6,14},{7,15},{8,0},{9,1},... | collective-permute-start | bytes 393224 | tf_op jit(solution)/shard_map/ppermute | solution.py:311
  4.0 3.6 %collective-permute-start.4 = (f32[2,128,128]{2,1,0:T(8,128)}, f32[2,128,128]{2,1,0:T(8,128)S(1)}, u32[]{:S(2)}, u32[]{:S(2)}) collective-permute-start(f32[2,128,128]{2,1,0:T(8,128)} %own.3), channel_id=1, source_target_pairs={{7,0},{10,1},{9,2},{14,5},{13,6},{0,7},{15,8},{2,9},{1,10},{6,13},... | collective-permute-start | bytes 393224 | tf_op jit(solution)/shard_map/ppermute | solution.py:312
  7.6 0.1 collective-permute-start.1
  7.7 4.3 %collective-permute-start = (f32[2,128,128]{2,1,0:T(8,128)}, f32[2,128,128]{2,1,0:T(8,128)}, u32[]{:S(2)}, u32[]{:S(2)}) collective-permute-start(f32[2,128,128]{2,1,0:T(8,128)} %own.3), channel_id=1, source_target_pairs={{15,0},{2,1},{1,2},{6,5},{5,6},{8,7},{7,8},{10,9},{9,10},{14,13},{... | collective-permute-start | bytes 393224 | tf_op jit(solution)/shard_map/ppermute | solution.py:314
  12.0 0.0 collective-permute-done.2.partner
  12.0 0.1 collective-permute-start.3
  12.1 1.5 %prepare.1 = (bf16[384,1152]{1,0:T(8,128)(2,1)S(1)}, bf16[320,384]{1,0:T(8,128)(2,1)S(1)}, bf16[768,240]{1,0:T(8,128)(2,1)S(1)}) custom-call(f32[3,3,128,128]{3,2,1,0:T(8,128)} %conv_hbm.1, f32[320,128]{1,0:T(8,128)} %lift_hbm.1, f32[3,3,3,32,40]{4,3,2,1,0:T(8,128)} %vol_hbm.1), custom_call_target="tpu_custom_call" | custom-call | flops 99999997952 | bytes 99999997952 | tf_op jit(solution)/shard_map/prepare/pallas_call | solution.py:231
  13.7 0.1 pad_add_fusion.flags
  13.8 0.0 collective-permute-done.4.partner_far
  13.8 0.0 collective-permute-done.1.own_mate
  13.8 0.0 collective-permute-done.3.partner_mate
  13.8 0.0 copy-done
  13.8 4.5 %near.1 = (f32[24,192,256]{2,1,0:T(8,128)S(1)}, f32[640,128]{1,0:T(8,128)S(1)}) custom-call(s32[4]{0:T(128)S(1)} %pad_add_fusion.flags, f32[2,128,128]{2,1,0:T(8,128)S(1)} %copy-done, f32[2,128,128]{2,1,0:T(8,128)S(1)} %collective-permute-done.1.own_mate, f32[2,128,128]{2,1,0:T(8,128)S(1)} %collective-permute-done.2.partner, ...), custom_call_target="tpu_custom_call" | custom-call | flops 99999997952 | bytes 99999997952 | tf_op jit(solution)/shard_map/near/pallas_call | solution.py:231
  18.3 0.0 collective-permute-done.own_far
  18.3 5.8 %far.1 = f32[64,48,128]{2,1,0:T(8,128)} custom-call(s32[4]{0:T(128)S(1)} %pad_add_fusion.flags, f32[2,128,128]{2,1,0:T(8,128)S(1)} %copy-done, f32[2,128,128]{2,1,0:T(8,128)} %collective-permute-done.own_far, f32[640,128]{1,0:T(8,128)S(1)} %get-tuple-element.13.other, bf16[384,1152]{1,0:T(8,128)(2,1)S(1)} %get-tuple-element.10.conv, ...), custom_call_target="tpu_custom_call" | custom-call | flops 99999997952 | bytes 99999997952 | tf_op jit(solution)/shard_map/far/pallas_call | solution.py:231
Async XLA Ops:
  0.0 13.8 %copy-start = (f32[2,128,128]{2,1,0:T(8,128)S(1)}, f32[2,128,128]{2,1,0:T(8,128)}, u32[]{:S(2)}) copy-start(f32[2,128,128]{2,1,0:T(8,128)} %own.3) | copy-start | bytes 393220
  0.0 12.0 %collective-permute-start.2 = (f32[2,128,128]{2,1,0:T(8,128)}, f32[2,128,128]{2,1,0:T(8,128)S(1)}, u32[]{:S(2)}, u32[]{:S(2)}) collective-permute-start(f32[2,128,128]{2,1,0:T(8,128)} %own.3), channel_id=1, source_target_pairs={{0,8},{1,9},{2,10},{3,11},{4,12},{5,13},{6,14},{7,15},{8,0},{9,1},... | collective-permute-start | bytes 393224 | tf_op jit(solution)/shard_map/ppermute | solution.py:311
  4.0 9.7 %collective-permute-start.4 = (f32[2,128,128]{2,1,0:T(8,128)}, f32[2,128,128]{2,1,0:T(8,128)S(1)}, u32[]{:S(2)}, u32[]{:S(2)}) collective-permute-start(f32[2,128,128]{2,1,0:T(8,128)} %own.3), channel_id=1, source_target_pairs={{7,0},{10,1},{9,2},{14,5},{13,6},{0,7},{15,8},{2,9},{1,10},{6,13},... | collective-permute-start | bytes 393224 | tf_op jit(solution)/shard_map/ppermute | solution.py:312
  7.6 6.1 %collective-permute-start.1 = (f32[2,128,128]{2,1,0:T(8,128)}, f32[2,128,128]{2,1,0:T(8,128)S(1)}, u32[]{:S(2)}, u32[]{:S(2)}) collective-permute-start(f32[2,128,128]{2,1,0:T(8,128)} %own.3), channel_id=1, source_target_pairs={{0,1},{1,0},{2,3},{3,2},{4,5},{5,4},{6,7},{7,6},{8,9},{9,8},{10,11... | collective-permute-start | bytes 393224 | tf_op jit(solution)/shard_map/ppermute | solution.py:313
  7.7 10.6 %collective-permute-start = (f32[2,128,128]{2,1,0:T(8,128)}, f32[2,128,128]{2,1,0:T(8,128)}, u32[]{:S(2)}, u32[]{:S(2)}) collective-permute-start(f32[2,128,128]{2,1,0:T(8,128)} %own.3), channel_id=1, source_target_pairs={{15,0},{2,1},{1,2},{6,5},{5,6},{8,7},{7,8},{10,9},{9,10},{14,13},{... | collective-permute-start | bytes 393224 | tf_op jit(solution)/shard_map/ppermute | solution.py:314
  12.0 1.7 %collective-permute-start.3 = (f32[2,128,128]{2,1,0:T(8,128)S(1)}, f32[2,128,128]{2,1,0:T(8,128)S(1)}, u32[]{:S(2)}, u32[]{:S(2)}) collective-permute-start(f32[2,128,128]{2,1,0:T(8,128)S(1)} %collective-permute-done.2.partner), channel_id=1, source_target_pairs={{0,1},{1,0},{2,3},{3,2},{4,5},{5,4},{6,7},{7,6},{8,9},{9,8},{10,11... | collective-permute-start | bytes 393224 | tf_op jit(solution)/shard_map/ppermute | solution.py:315

commit v5 on v4

--- a/solution.py
+++ b/solution.py
@@ -9,7 +9,8 @@
 DISP = 48
 STEP = 8
 CHUNK = 24
-COST = 10**11
+COST = 10**10
+BYTES = 10**7
 F32 = jnp.float32
 BF16 = jnp.bfloat16
 VMEM_BYTES = 24 * 1024 * 1024
@@ -68,7 +69,7 @@
     return [jnp.logical_or(half != k, flags[2 + k] == 1) for k in range(2)]
 
 
-def prepare_kernel(conv_hbm, lift_hbm, vol_hbm, conv_out, lift_out, banded, conv, lift, vol, sems):
+def prepare_kernel(conv_hbm, lift_hbm, vol_hbm, mate, conv_out, lift_out, banded, conv, lift, vol, sems):
     pairs = ((conv_hbm, conv), (lift_hbm, lift), (vol_hbm, vol))
     copies = [pltpu.make_async_copy(a, b, sems.at[i]) for i, (a, b) in enumerate(pairs)]
     for copy in copies:
@@ -174,13 +175,12 @@
         yield d, y[:m] + (y[m:] + mm(weight[:m], low))
 
 
-def near_kernel(flags, own, own_mate, partner, partner_mate, partner_far, conv, lift, banded, part, far_other, anchor, other, moved, shifted, c_high, c_low):
+def near_kernel(flags, own, own_mate, partner, partner_mate, conv, lift, banded, part, anchor, other, moved, shifted, c_high, c_low):
     half = 1 - flags[1]
     right = flags[0] == 1
     per = lift.shape[0] // GROUPS
-    fours = [four_rows(half, own, own_mate), four_rows(half, partner, partner_mate), four_rows(1 - half, partner, partner_far)]
-    insides = [rows_inside(flags, half)] * 2 + [rows_inside(flags, 1 - half)]
-    features(fours, conv, lift, [anchor, other, far_other], insides)
+    fours = [four_rows(half, own, own_mate), four_rows(half, partner, partner_mate)]
+    features(fours, conv, lift, [anchor, other], [rows_inside(flags, half)] * 2)
     move_anchor(right, anchor, moved, per)
     move_other(right, other, shifted, per)
     correlate(right, anchor, moved, other, shifted, c_high, c_low, per)
@@ -188,12 +188,13 @@
         part[d // 2] = y
 
 
-def far_kernel(flags, own, own_far, other, conv, lift, banded, part, result, anchor, moved, shifted, c_high, c_low, out, sems):
+def far_kernel(flags, own, own_far, partner, partner_far, conv, lift, banded, part, result, anchor, other, moved, shifted, c_high, c_low, out, sems):
     half = flags[1]
     right = flags[0] == 1
     per = lift.shape[0] // GROUPS
+    fours = [four_rows(half, own, own_far), four_rows(half, partner, partner_far)]
+    features(fours, conv, lift, [anchor, other], [rows_inside(flags, half)] * 2)
     move_other(right, other, shifted, per)
-    features([four_rows(half, own, own_far)], conv, lift, [anchor], [rows_inside(flags, half)])
     move_anchor(right, anchor, moved, per)
     correlate(right, anchor, moved, other, shifted, c_high, c_low, per)
     columns = own.shape[2]
@@ -235,19 +236,19 @@
         out_specs=jax.tree.map(lambda _: vmem(), out_shape) if out_specs is None else out_specs,
         scratch_shapes=scratch,
         compiler_params=pltpu.CompilerParams(vmem_limit_bytes=VMEM_BYTES),
-        cost_estimate=pl.CostEstimate(flops=COST, bytes_accessed=COST, transcendentals=0),
+        cost_estimate=pl.CostEstimate(flops=COST, bytes_accessed=BYTES, transcendentals=0),
         name=name,
     )(*args)
 
 
-def prepare(conv, lift, vol):
+def prepare(conv, lift, vol, mate):
     channels = conv.shape[2]
     feats = lift.shape[0]
     shapes = [(3 * channels, 9 * channels), (feats, 3 * channels), (8 * 3 * vol.shape[3], 6 * GROUPS)]
     out = [jax.ShapeDtypeStruct(s, BF16) for s in shapes]
     scratch = [pltpu.VMEM(x.shape, F32) for x in (conv, lift, vol)] + [pltpu.SemaphoreType.DMA((3,))]
     args = [pltpu.with_memory_space_constraint(x, pltpu.HBM) for x in (conv, lift, vol)]
-    return call(prepare_kernel, "prepare", out, [hbm()] * 3, scratch, *args)
+    return call(prepare_kernel, "prepare", out, [hbm()] * 3 + [pl.BlockSpec(memory_space=pl.ANY)], scratch, *args, mate)
 
 
 def sizes(operands, columns):
@@ -260,21 +261,21 @@
     return plain, moved, shifted, volume, part
 
 
-def near(flags, own, own_mate, partner, partner_mate, partner_far, operands):
+def near(flags, own, own_mate, partner, partner_mate, operands):
     plain, moved, shifted, volume, part = sizes(operands, own.shape[2])
     scratch = [pltpu.VMEM(s, F32) for s in (plain, plain, moved, shifted)] + [pltpu.VMEM(volume, BF16)] * 2
-    args = (own, own_mate, partner, partner_mate, partner_far, *operands)
-    out = [jax.ShapeDtypeStruct(s, F32) for s in (part, plain)]
+    args = (own, own_mate, partner, partner_mate, *operands)
+    out = jax.ShapeDtypeStruct(part, F32)
     return call(near_kernel, "near", out, [smem()] + [vmem()] * len(args), scratch, flags, *args)
 
 
-def far(flags, own, own_far, other, operands, part):
+def far(flags, own, own_far, partner, partner_far, operands, part):
     columns = own.shape[2]
     plain, moved, shifted, volume, _ = sizes(operands, columns)
     rows = operands[2].shape[0] // 12
-    scratch = [pltpu.VMEM(s, F32) for s in (plain, moved, shifted)] + [pltpu.VMEM(volume, BF16)] * 2
+    scratch = [pltpu.VMEM(s, F32) for s in (plain, plain, moved, shifted)] + [pltpu.VMEM(volume, BF16)] * 2
     scratch += [pltpu.VMEM((rows * DISP, columns), F32), pltpu.SemaphoreType.DMA((1 + DISP // CHUNK,))]
-    args = (own, own_far, other, *operands, part)
+    args = (own, own_far, partner, partner_far, *operands, part)
     in_specs = [smem()] + [vmem()] * len(args)
     out = jax.ShapeDtypeStruct((rows, DISP, columns), F32)
     return call(far_kernel, "far", out, in_specs, scratch, flags, *args, out_specs=hbm())
@@ -313,9 +314,9 @@
     own_mate = lax.ppermute(images, "rows", mates)
     own_far = lax.ppermute(images, "rows", beyond)
     partner_mate = lax.ppermute(partner, "rows", mates)
-    operands = prepare(conv_weight, lift_weight, vol_weight)
-    part, other = near(flags, images, own_mate, partner, partner_mate, partner_far, operands)
-    whole = far(flags, images, own_far, other, operands, part)
+    operands = prepare(conv_weight, lift_weight, vol_weight, own_mate)
+    part = near(flags, images, own_mate, partner, partner_mate, operands)
+    whole = far(flags, images, own_far, partner, partner_far, operands, part)
     rows, _, columns = images.shape
     return whole.reshape(rows, vol_weight.shape[3], DISP, columns)
 

time: 24.4 us -> 23.7 us (0.971)
  starting transfers between devices: 12.1 us -> 10.6 us
  waiting for transfers between devices: 0.01 us -> 1.05 us
    ppermute x1, starting transfers between devices: 4.3 us -> 1.92 us  [on_device(): own_far = lax.ppermute(images, 'rows', beyond)]
    ppermute x1, waiting for transfers between devices: 0.01 us -> 1.04 us  [on_device(): own_far = lax.ppermute(images, 'rows', beyond)]
    ppermute x1, starting transfers between devices: 3.59 us -> 4.54 us  [on_device(): partner_far = lax.ppermute(images, 'rows', beyond_partner)]
  transfers between devices with their start and end apart: 5 -> 5, of which waited for: 0 -> 1; matrix products, arithmetic and copies ran while one was open for 0% -> 0% of each run, Pallas kernels for 25% -> 26%
where the time goes in v5:
time: 23.7 us; the launch traced here: 23.5 us
  Pallas kernels  11.7 us (49%)
  starting transfers between devices  10.6 us (45%)
  waiting for transfers between devices  1.05 us (4%)
    pallas_call x3, Pallas kernels, call(): pl.pallas_call(kernel, out_shape=out_shape, in_specs=in_specs, out_specs=...  11.7 us
    ppermute x1, starting transfers between devices, on_device(): partner_far = lax.ppermute(images, 'rows', beyond_partner)  4.54 us
    ppermute x1, starting transfers between devices, on_device(): partner = lax.ppermute(images, 'rows', swap)  4.04 us
    ppermute x1, starting transfers between devices, on_device(): own_far = lax.ppermute(images, 'rows', beyond)  1.92 us
    ppermute x1, waiting for transfers between devices, on_device(): own_far = lax.ppermute(images, 'rows', beyond)  1.04 us
  transfers between devices with their start and end apart: 5, of which 1 were waited for; matrix products, arithmetic and copies ran while one was open for 0% of the time, Pallas kernels for 26%

profile of v5, /device:TPU:0, one launch (start us, length us, event | category | flops | bytes accessed | tf_op | source)
XLA Modules:
  0.0 23.5 jit_solution(2907570162564438818)
XLA Ops:
  0.0 4.0 %collective-permute-start.1 = (f32[2,128,128]{2,1,0:T(8,128)}, f32[2,128,128]{2,1,0:T(8,128)S(1)}, u32[]{:S(2)}, u32[]{:S(2)}) collective-permute-start(f32[2,128,128]{2,1,0:T(8,128)} %own.3), channel_id=1, source_target_pairs={{0,8},{1,9},{2,10},{3,11},{4,12},{5,13},{6,14},{7,15},{8,0},{9,1},... | collective-permute-start | bytes 393224 | tf_op jit(solution)/shard_map/ppermute | solution.py:312
  4.0 0.0 collective-permute-start.3
  4.0 4.5 %collective-permute-start.2 = (f32[2,128,128]{2,1,0:T(8,128)}, f32[2,128,128]{2,1,0:T(8,128)S(1)}, u32[]{:S(2)}, u32[]{:S(2)}) collective-permute-start(f32[2,128,128]{2,1,0:T(8,128)} %own.3), channel_id=1, source_target_pairs={{7,0},{10,1},{9,2},{14,5},{13,6},{0,7},{15,8},{2,9},{1,10},{6,13},... | collective-permute-start | bytes 393224 | tf_op jit(solution)/shard_map/ppermute | solution.py:313
  8.6 1.9 %collective-permute-start = (f32[2,128,128]{2,1,0:T(8,128)}, f32[2,128,128]{2,1,0:T(8,128)S(1)}, u32[]{:S(2)}, u32[]{:S(2)}) collective-permute-start(f32[2,128,128]{2,1,0:T(8,128)} %own.3), channel_id=1, source_target_pairs={{15,0},{2,1},{1,2},{6,5},{5,6},{8,7},{7,8},{10,9},{9,10},{14,13},{... | collective-permute-start | bytes 393224 | tf_op jit(solution)/shard_map/ppermute | solution.py:315
  10.6 0.1 pad_add_fusion.flags
  10.6 0.0 copy-start
  10.6 0.0 collective-permute-done.1.partner
  10.6 0.0 collective-permute-start.4
  10.7 0.0 collective-permute-done.3.mate.own_mate
  10.7 1.5 %prepare.1 = (bf16[384,1152]{1,0:T(8,128)(2,1)S(1)}, bf16[320,384]{1,0:T(8,128)(2,1)S(1)}, bf16[768,240]{1,0:T(8,128)(2,1)S(1)}) custom-call(f32[3,3,128,128]{3,2,1,0:T(8,128)} %conv_hbm.1, f32[320,128]{1,0:T(8,128)} %lift_hbm.1, f32[3,3,3,32,40]{4,3,2,1,0:T(8,128)} %vol_hbm.1, f32[2,128,128]{2,1,0:T(8,128)S(1)} %collective-permute-done.3.mate.own_mate), custom_call_target="tpu_custom_call" | custom-call | flops 10000000000 | bytes 10000000 | tf_op jit(solution)/shard_map/prepare/pallas_call | solution.py:232
  12.2 0.0 collective-permute-done.4.partner_mate
  12.3 0.0 copy-done
  12.3 4.5 %near.1.part = f32[24,192,256]{2,1,0:T(8,128)S(1)} custom-call(s32[4]{0:T(128)S(1)} %pad_add_fusion.flags, f32[2,128,128]{2,1,0:T(8,128)S(1)} %copy-done, f32[2,128,128]{2,1,0:T(8,128)S(1)} %collective-permute-done.3.mate.own_mate, f32[2,128,128]{2,1,0:T(8,128)S(1)} %collective-permute-done.1.partner, ...), custom_call_target="tpu_custom_call" | custom-call | flops 10000000000 | bytes 10000000 | tf_op jit(solution)/shard_map/near/pallas_call | solution.py:232
  16.7 0.0 collective-permute-done.2.partner_far
  16.7 1.0 %collective-permute-done.own_far = f32[2,128,128]{2,1,0:T(8,128)S(1)} collective-permute-done((f32[2,128,128]{2,1,0:T(8,128)}, f32[2,128,128]{2,1,0:T(8,128)S(1)}, u32[]{:S(2)}, u32[]{:S(2)}) %collective-permute-start) | collective-permute-done | bytes 131104 | tf_op jit(solution)/shard_map/ppermute | solution.py:315
  17.8 5.7 %far.1 = f32[64,48,128]{2,1,0:T(8,128)} custom-call(s32[4]{0:T(128)S(1)} %pad_add_fusion.flags, f32[2,128,128]{2,1,0:T(8,128)S(1)} %copy-done, f32[2,128,128]{2,1,0:T(8,128)S(1)} %collective-permute-done.own_far, f32[2,128,128]{2,1,0:T(8,128)S(1)} %collective-permute-done.1.partner, f32[2,128,128]{2,1,0:T(8,128)S(1)} %collective-permute-done.2.partner_far, ...), custom_call_target="tpu_custom_call" | custom-call | flops 10000000000 | bytes 10000000 | tf_op jit(solution)/shard_map/far/pallas_call | solution.py:232
Async XLA Ops:
  0.0 10.6 %collective-permute-start.1 = (f32[2,128,128]{2,1,0:T(8,128)}, f32[2,128,128]{2,1,0:T(8,128)S(1)}, u32[]{:S(2)}, u32[]{:S(2)}) collective-permute-start(f32[2,128,128]{2,1,0:T(8,128)} %own.3), channel_id=1, source_target_pairs={{0,8},{1,9},{2,10},{3,11},{4,12},{5,13},{6,14},{7,15},{8,0},{9,1},... | collective-permute-start | bytes 393224 | tf_op jit(solution)/shard_map/ppermute | solution.py:312
  4.0 6.7 %collective-permute-start.3 = (f32[2,128,128]{2,1,0:T(8,128)}, f32[2,128,128]{2,1,0:T(8,128)S(1)}, u32[]{:S(2)}, u32[]{:S(2)}) collective-permute-start(f32[2,128,128]{2,1,0:T(8,128)} %own.3), channel_id=1, source_target_pairs={{0,1},{1,0},{2,3},{3,2},{4,5},{5,4},{6,7},{7,6},{8,9},{9,8},{10,11... | collective-permute-start | bytes 393224 | tf_op jit(solution)/shard_map/ppermute | solution.py:314
  4.0 12.7 %collective-permute-start.2 = (f32[2,128,128]{2,1,0:T(8,128)}, f32[2,128,128]{2,1,0:T(8,128)S(1)}, u32[]{:S(2)}, u32[]{:S(2)}) collective-permute-start(f32[2,128,128]{2,1,0:T(8,128)} %own.3), channel_id=1, source_target_pairs={{7,0},{10,1},{9,2},{14,5},{13,6},{0,7},{15,8},{2,9},{1,10},{6,13},... | collective-permute-start | bytes 393224 | tf_op jit(solution)/shard_map/ppermute | solution.py:313
  8.6 9.2 %collective-permute-start = (f32[2,128,128]{2,1,0:T(8,128)}, f32[2,128,128]{2,1,0:T(8,128)S(1)}, u32[]{:S(2)}, u32[]{:S(2)}) collective-permute-start(f32[2,128,128]{2,1,0:T(8,128)} %own.3), channel_id=1, source_target_pairs={{15,0},{2,1},{1,2},{6,5},{5,6},{8,7},{7,8},{10,9},{9,10},{14,13},{... | collective-permute-start | bytes 393224 | tf_op jit(solution)/shard_map/ppermute | solution.py:315
  10.6 1.6 %copy-start = (f32[2,128,128]{2,1,0:T(8,128)S(1)}, f32[2,128,128]{2,1,0:T(8,128)}, u32[]{:S(2)}) copy-start(f32[2,128,128]{2,1,0:T(8,128)} %own.3) | copy-start | bytes 393220
  10.6 1.6 %collective-permute-start.4 = (f32[2,128,128]{2,1,0:T(8,128)S(1)}, f32[2,128,128]{2,1,0:T(8,128)S(1)}, u32[]{:S(2)}, u32[]{:S(2)}) collective-permute-start(f32[2,128,128]{2,1,0:T(8,128)S(1)} %collective-permute-done.1.partner), channel_id=1, source_target_pairs={{0,1},{1,0},{2,3},{3,2},{4,5},{5,4},{6,7},{7,6},{8,9},{9,8},{10,11... | collective-permute-start | bytes 393224 | tf_op jit(solution)/shard_map/ppermute | solution.py:316

commit v6 on v5

--- a/solution.py
+++ b/solution.py
@@ -8,7 +8,7 @@
 GROUPS = 40
 DISP = 48
 STEP = 8
-CHUNK = 24
+CHUNK = 16
 COST = 10**10
 BYTES = 10**7
 F32 = jnp.float32

time: 23.7 us -> 23.6 us (level)
  no operation moved by 1% of the time
where the time goes in v6:
time: 23.6 us; the launch traced here: 23.4 us
  Pallas kernels  11.6 us (49%)
  starting transfers between devices  10.6 us (45%)
  waiting for transfers between devices  1.05 us (4%)
    pallas_call x3, Pallas kernels, call(): pl.pallas_call(kernel, out_shape=out_shape, in_specs=in_specs, out_specs=...  11.6 us
    ppermute x1, starting transfers between devices, on_device(): partner_far = lax.ppermute(images, 'rows', beyond_partner)  4.54 us
    ppermute x1, starting transfers between devices, on_device(): partner = lax.ppermute(images, 'rows', swap)  4.04 us
    ppermute x1, starting transfers between devices, on_device(): own_far = lax.ppermute(images, 'rows', beyond)  1.92 us
    ppermute x1, waiting for transfers between devices, on_device(): own_far = lax.ppermute(images, 'rows', beyond)  1.04 us
  transfers between devices with their start and end apart: 5, of which 1 were waited for; matrix products, arithmetic and copies ran while one was open for 0% of the time, Pallas kernels for 26%

profile of v6, /device:TPU:0, one launch (start us, length us, event | category | flops | bytes accessed | tf_op | source)
XLA Modules:
  0.0 23.4 jit_solution(5078502694810883344)
XLA Ops:
  0.0 4.0 %collective-permute-start.1 = (f32[2,128,128]{2,1,0:T(8,128)}, f32[2,128,128]{2,1,0:T(8,128)S(1)}, u32[]{:S(2)}, u32[]{:S(2)}) collective-permute-start(f32[2,128,128]{2,1,0:T(8,128)} %own.3), channel_id=1, source_target_pairs={{0,8},{1,9},{2,10},{3,11},{4,12},{5,13},{6,14},{7,15},{8,0},{9,1},... | collective-permute-start | bytes 393224 | tf_op jit(solution)/shard_map/ppermute | solution.py:312
  4.0 0.0 collective-permute-start.3
  4.0 4.5 %collective-permute-start.2 = (f32[2,128,128]{2,1,0:T(8,128)}, f32[2,128,128]{2,1,0:T(8,128)S(1)}, u32[]{:S(2)}, u32[]{:S(2)}) collective-permute-start(f32[2,128,128]{2,1,0:T(8,128)} %own.3), channel_id=1, source_target_pairs={{7,0},{10,1},{9,2},{14,5},{13,6},{0,7},{15,8},{2,9},{1,10},{6,13},... | collective-permute-start | bytes 393224 | tf_op jit(solution)/shard_map/ppermute | solution.py:313
  8.6 1.9 %collective-permute-start = (f32[2,128,128]{2,1,0:T(8,128)}, f32[2,128,128]{2,1,0:T(8,128)S(1)}, u32[]{:S(2)}, u32[]{:S(2)}) collective-permute-start(f32[2,128,128]{2,1,0:T(8,128)} %own.3), channel_id=1, source_target_pairs={{15,0},{2,1},{1,2},{6,5},{5,6},{8,7},{7,8},{10,9},{9,10},{14,13},{... | collective-permute-start | bytes 393224 | tf_op jit(solution)/shard_map/ppermute | solution.py:315
  10.6 0.1 pad_add_fusion.flags
  10.6 0.0 copy-start
  10.6 0.0 collective-permute-done.1.partner
  10.6 0.0 collective-permute-start.4
  10.7 0.0 collective-permute-done.3.mate.own_mate
  10.7 1.5 %prepare.1 = (bf16[384,1152]{1,0:T(8,128)(2,1)S(1)}, bf16[320,384]{1,0:T(8,128)(2,1)S(1)}, bf16[768,240]{1,0:T(8,128)(2,1)S(1)}) custom-call(f32[3,3,128,128]{3,2,1,0:T(8,128)} %conv_hbm.1, f32[320,128]{1,0:T(8,128)} %lift_hbm.1, f32[3,3,3,32,40]{4,3,2,1,0:T(8,128)} %vol_hbm.1, f32[2,128,128]{2,1,0:T(8,128)S(1)} %collective-permute-done.3.mate.own_mate), custom_call_target="tpu_custom_call" | custom-call | flops 10000000000 | bytes 10000000 | tf_op jit(solution)/shard_map/prepare/pallas_call | solution.py:232
  12.2 0.0 collective-permute-done.4.partner_mate
  12.3 0.0 copy-done
  12.3 4.5 %near.1.part = f32[24,192,256]{2,1,0:T(8,128)S(1)} custom-call(s32[4]{0:T(128)S(1)} %pad_add_fusion.flags, f32[2,128,128]{2,1,0:T(8,128)S(1)} %copy-done, f32[2,128,128]{2,1,0:T(8,128)S(1)} %collective-permute-done.3.mate.own_mate, f32[2,128,128]{2,1,0:T(8,128)S(1)} %collective-permute-done.1.partner, ...), custom_call_target="tpu_custom_call" | custom-call | flops 10000000000 | bytes 10000000 | tf_op jit(solution)/shard_map/near/pallas_call | solution.py:232
  16.7 0.0 collective-permute-done.2.partner_far
  16.7 1.0 %collective-permute-done.own_far = f32[2,128,128]{2,1,0:T(8,128)S(1)} collective-permute-done((f32[2,128,128]{2,1,0:T(8,128)}, f32[2,128,128]{2,1,0:T(8,128)S(1)}, u32[]{:S(2)}, u32[]{:S(2)}) %collective-permute-start) | collective-permute-done | bytes 131104 | tf_op jit(solution)/shard_map/ppermute | solution.py:315
  17.8 5.6 %far.1 = f32[64,48,128]{2,1,0:T(8,128)} custom-call(s32[4]{0:T(128)S(1)} %pad_add_fusion.flags, f32[2,128,128]{2,1,0:T(8,128)S(1)} %copy-done, f32[2,128,128]{2,1,0:T(8,128)S(1)} %collective-permute-done.own_far, f32[2,128,128]{2,1,0:T(8,128)S(1)} %collective-permute-done.1.partner, f32[2,128,128]{2,1,0:T(8,128)S(1)} %collective-permute-done.2.partner_far, ...), custom_call_target="tpu_custom_call" | custom-call | flops 10000000000 | bytes 10000000 | tf_op jit(solution)/shard_map/far/pallas_call | solution.py:232
Async XLA Ops:
  0.0 10.6 %collective-permute-start.1 = (f32[2,128,128]{2,1,0:T(8,128)}, f32[2,128,128]{2,1,0:T(8,128)S(1)}, u32[]{:S(2)}, u32[]{:S(2)}) collective-permute-start(f32[2,128,128]{2,1,0:T(8,128)} %own.3), channel_id=1, source_target_pairs={{0,8},{1,9},{2,10},{3,11},{4,12},{5,13},{6,14},{7,15},{8,0},{9,1},... | collective-permute-start | bytes 393224 | tf_op jit(solution)/shard_map/ppermute | solution.py:312
  4.0 6.7 %collective-permute-start.3 = (f32[2,128,128]{2,1,0:T(8,128)}, f32[2,128,128]{2,1,0:T(8,128)S(1)}, u32[]{:S(2)}, u32[]{:S(2)}) collective-permute-start(f32[2,128,128]{2,1,0:T(8,128)} %own.3), channel_id=1, source_target_pairs={{0,1},{1,0},{2,3},{3,2},{4,5},{5,4},{6,7},{7,6},{8,9},{9,8},{10,11... | collective-permute-start | bytes 393224 | tf_op jit(solution)/shard_map/ppermute | solution.py:314
  4.0 12.7 %collective-permute-start.2 = (f32[2,128,128]{2,1,0:T(8,128)}, f32[2,128,128]{2,1,0:T(8,128)S(1)}, u32[]{:S(2)}, u32[]{:S(2)}) collective-permute-start(f32[2,128,128]{2,1,0:T(8,128)} %own.3), channel_id=1, source_target_pairs={{7,0},{10,1},{9,2},{14,5},{13,6},{0,7},{15,8},{2,9},{1,10},{6,13},... | collective-permute-start | bytes 393224 | tf_op jit(solution)/shard_map/ppermute | solution.py:313
  8.6 9.2 %collective-permute-start = (f32[2,128,128]{2,1,0:T(8,128)}, f32[2,128,128]{2,1,0:T(8,128)S(1)}, u32[]{:S(2)}, u32[]{:S(2)}) collective-permute-start(f32[2,128,128]{2,1,0:T(8,128)} %own.3), channel_id=1, source_target_pairs={{15,0},{2,1},{1,2},{6,5},{5,6},{8,7},{7,8},{10,9},{9,10},{14,13},{... | collective-permute-start | bytes 393224 | tf_op jit(solution)/shard_map/ppermute | solution.py:315
  10.6 1.6 %copy-start = (f32[2,128,128]{2,1,0:T(8,128)S(1)}, f32[2,128,128]{2,1,0:T(8,128)}, u32[]{:S(2)}) copy-start(f32[2,128,128]{2,1,0:T(8,128)} %own.3) | copy-start | bytes 393220
  10.6 1.6 %collective-permute-start.4 = (f32[2,128,128]{2,1,0:T(8,128)S(1)}, f32[2,128,128]{2,1,0:T(8,128)S(1)}, u32[]{:S(2)}, u32[]{:S(2)}) collective-permute-start(f32[2,128,128]{2,1,0:T(8,128)S(1)} %collective-permute-done.1.partner), channel_id=1, source_target_pairs={{0,1},{1,0},{2,3},{3,2},{4,5},{5,4},{6,7},{7,6},{8,9},{9,8},{10,11... | collective-permute-start | bytes 393224 | tf_op jit(solution)/shard_map/ppermute | solution.py:316

commit v7 on v6

--- a/solution.py
+++ b/solution.py
@@ -8,7 +8,7 @@
 GROUPS = 40
 DISP = 48
 STEP = 8
-CHUNK = 16
+LAST = 8
 COST = 10**10
 BYTES = 10**7
 F32 = jnp.float32
@@ -207,10 +207,10 @@
             for row in range(2):
                 o = from_columns(y[row * 3 * outs : (row + 1) * 3 * outs, k * columns : (k + 1) * columns], outs)
                 out[pl.ds(row * outs * DISP + d + k, outs, stride=DISP)] = o
-        if (d + 2) % CHUNK == 0:
-            i = d // CHUNK
-            at = (slice(None), pl.ds(i * CHUNK, CHUNK))
-            copies.append(pltpu.make_async_copy(out.reshape(rows, DISP, columns).at[at], result.at[at], sems.at[1 + i]))
+        if d + 2 in (DISP - LAST, DISP):
+            i = len(copies)
+            at = (slice(None), pl.ds(DISP - LAST, LAST) if i else pl.ds(0, DISP - LAST))
+            copies.append(pltpu.make_async_copy(out.reshape(rows, DISP, columns).at[at], result.at[at], sems.at[i]))
             copies[-1].start()
     for copy in copies:
         copy.wait()
@@ -274,7 +274,7 @@
     plain, moved, shifted, volume, _ = sizes(operands, columns)
     rows = operands[2].shape[0] // 12
     scratch = [pltpu.VMEM(s, F32) for s in (plain, plain, moved, shifted)] + [pltpu.VMEM(volume, BF16)] * 2
-    scratch += [pltpu.VMEM((rows * DISP, columns), F32), pltpu.SemaphoreType.DMA((1 + DISP // CHUNK,))]
+    scratch += [pltpu.VMEM((rows * DISP, columns), F32), pltpu.SemaphoreType.DMA((2,))]
     args = (own, own_far, partner, partner_far, *operands, part)
     in_specs = [smem()] + [vmem()] * len(args)
     out = jax.ShapeDtypeStruct((rows, DISP, columns), F32)

time: 23.6 us -> 23.6 us (level)
  no operation moved by 1% of the time
where the time goes in v7:
time: 23.6 us; the launch traced here: 23.4 us
  Pallas kernels  11.6 us (49%)
  starting transfers between devices  10.6 us (45%)
  waiting for transfers between devices  1.05 us (4%)
    pallas_call x3, Pallas kernels, call(): pl.pallas_call(kernel, out_shape=out_shape, in_specs=in_specs, out_specs=...  11.6 us
    ppermute x1, starting transfers between devices, on_device(): partner_far = lax.ppermute(images, 'rows', beyond_partner)  4.54 us
    ppermute x1, starting transfers between devices, on_device(): partner = lax.ppermute(images, 'rows', swap)  4.04 us
    ppermute x1, starting transfers between devices, on_device(): own_far = lax.ppermute(images, 'rows', beyond)  1.92 us
    ppermute x1, waiting for transfers between devices, on_device(): own_far = lax.ppermute(images, 'rows', beyond)  1.04 us
  transfers between devices with their start and end apart: 5, of which 1 were waited for; matrix products, arithmetic and copies ran while one was open for 0% of the time, Pallas kernels for 26%

profile of v7, /device:TPU:0, one launch (start us, length us, event | category | flops | bytes accessed | tf_op | source)
XLA Modules:
  0.0 23.4 jit_solution(6027971491372872368)
XLA Ops:
  0.0 4.0 %collective-permute-start.1 = (f32[2,128,128]{2,1,0:T(8,128)}, f32[2,128,128]{2,1,0:T(8,128)S(1)}, u32[]{:S(2)}, u32[]{:S(2)}) collective-permute-start(f32[2,128,128]{2,1,0:T(8,128)} %own.3), channel_id=1, source_target_pairs={{0,8},{1,9},{2,10},{3,11},{4,12},{5,13},{6,14},{7,15},{8,0},{9,1},... | collective-permute-start | bytes 393224 | tf_op jit(solution)/shard_map/ppermute | solution.py:312
  4.0 0.0 collective-permute-start.3
  4.0 4.5 %collective-permute-start.2 = (f32[2,128,128]{2,1,0:T(8,128)}, f32[2,128,128]{2,1,0:T(8,128)S(1)}, u32[]{:S(2)}, u32[]{:S(2)}) collective-permute-start(f32[2,128,128]{2,1,0:T(8,128)} %own.3), channel_id=1, source_target_pairs={{7,0},{10,1},{9,2},{14,5},{13,6},{0,7},{15,8},{2,9},{1,10},{6,13},... | collective-permute-start | bytes 393224 | tf_op jit(solution)/shard_map/ppermute | solution.py:313
  8.6 1.9 %collective-permute-start = (f32[2,128,128]{2,1,0:T(8,128)}, f32[2,128,128]{2,1,0:T(8,128)S(1)}, u32[]{:S(2)}, u32[]{:S(2)}) collective-permute-start(f32[2,128,128]{2,1,0:T(8,128)} %own.3), channel_id=1, source_target_pairs={{15,0},{2,1},{1,2},{6,5},{5,6},{8,7},{7,8},{10,9},{9,10},{14,13},{... | collective-permute-start | bytes 393224 | tf_op jit(solution)/shard_map/ppermute | solution.py:315
  10.6 0.1 pad_add_fusion.flags
  10.6 0.0 copy-start
  10.6 0.0 collective-permute-done.1.partner
  10.6 0.0 collective-permute-start.4
  10.7 0.0 collective-permute-done.3.mate.own_mate
  10.7 1.5 %prepare.1 = (bf16[384,1152]{1,0:T(8,128)(2,1)S(1)}, bf16[320,384]{1,0:T(8,128)(2,1)S(1)}, bf16[768,240]{1,0:T(8,128)(2,1)S(1)}) custom-call(f32[3,3,128,128]{3,2,1,0:T(8,128)} %conv_hbm.1, f32[320,128]{1,0:T(8,128)} %lift_hbm.1, f32[3,3,3,32,40]{4,3,2,1,0:T(8,128)} %vol_hbm.1, f32[2,128,128]{2,1,0:T(8,128)S(1)} %collective-permute-done.3.mate.own_mate), custom_call_target="tpu_custom_call" | custom-call | flops 10000000000 | bytes 10000000 | tf_op jit(solution)/shard_map/prepare/pallas_call | solution.py:232
  12.2 0.0 collective-permute-done.4.partner_mate
  12.3 0.0 copy-done
  12.3 4.5 %near.1.part = f32[24,192,256]{2,1,0:T(8,128)S(1)} custom-call(s32[4]{0:T(128)S(1)} %pad_add_fusion.flags, f32[2,128,128]{2,1,0:T(8,128)S(1)} %copy-done, f32[2,128,128]{2,1,0:T(8,128)S(1)} %collective-permute-done.3.mate.own_mate, f32[2,128,128]{2,1,0:T(8,128)S(1)} %collective-permute-done.1.partner, ...), custom_call_target="tpu_custom_call" | custom-call | flops 10000000000 | bytes 10000000 | tf_op jit(solution)/shard_map/near/pallas_call | solution.py:232
  16.7 0.0 collective-permute-done.2.partner_far
  16.7 1.0 %collective-permute-done.own_far = f32[2,128,128]{2,1,0:T(8,128)S(1)} collective-permute-done((f32[2,128,128]{2,1,0:T(8,128)}, f32[2,128,128]{2,1,0:T(8,128)S(1)}, u32[]{:S(2)}, u32[]{:S(2)}) %collective-permute-start) | collective-permute-done | bytes 131104 | tf_op jit(solution)/shard_map/ppermute | solution.py:315
  17.8 5.6 %far.1 = f32[64,48,128]{2,1,0:T(8,128)} custom-call(s32[4]{0:T(128)S(1)} %pad_add_fusion.flags, f32[2,128,128]{2,1,0:T(8,128)S(1)} %copy-done, f32[2,128,128]{2,1,0:T(8,128)S(1)} %collective-permute-done.own_far, f32[2,128,128]{2,1,0:T(8,128)S(1)} %collective-permute-done.1.partner, f32[2,128,128]{2,1,0:T(8,128)S(1)} %collective-permute-done.2.partner_far, ...), custom_call_target="tpu_custom_call" | custom-call | flops 10000000000 | bytes 10000000 | tf_op jit(solution)/shard_map/far/pallas_call | solution.py:232
Async XLA Ops:
  0.0 10.6 %collective-permute-start.1 = (f32[2,128,128]{2,1,0:T(8,128)}, f32[2,128,128]{2,1,0:T(8,128)S(1)}, u32[]{:S(2)}, u32[]{:S(2)}) collective-permute-start(f32[2,128,128]{2,1,0:T(8,128)} %own.3), channel_id=1, source_target_pairs={{0,8},{1,9},{2,10},{3,11},{4,12},{5,13},{6,14},{7,15},{8,0},{9,1},... | collective-permute-start | bytes 393224 | tf_op jit(solution)/shard_map/ppermute | solution.py:312
  4.0 6.7 %collective-permute-start.3 = (f32[2,128,128]{2,1,0:T(8,128)}, f32[2,128,128]{2,1,0:T(8,128)S(1)}, u32[]{:S(2)}, u32[]{:S(2)}) collective-permute-start(f32[2,128,128]{2,1,0:T(8,128)} %own.3), channel_id=1, source_target_pairs={{0,1},{1,0},{2,3},{3,2},{4,5},{5,4},{6,7},{7,6},{8,9},{9,8},{10,11... | collective-permute-start | bytes 393224 | tf_op jit(solution)/shard_map/ppermute | solution.py:314
  4.0 12.7 %collective-permute-start.2 = (f32[2,128,128]{2,1,0:T(8,128)}, f32[2,128,128]{2,1,0:T(8,128)S(1)}, u32[]{:S(2)}, u32[]{:S(2)}) collective-permute-start(f32[2,128,128]{2,1,0:T(8,128)} %own.3), channel_id=1, source_target_pairs={{7,0},{10,1},{9,2},{14,5},{13,6},{0,7},{15,8},{2,9},{1,10},{6,13},... | collective-permute-start | bytes 393224 | tf_op jit(solution)/shard_map/ppermute | solution.py:313
  8.6 9.2 %collective-permute-start = (f32[2,128,128]{2,1,0:T(8,128)}, f32[2,128,128]{2,1,0:T(8,128)S(1)}, u32[]{:S(2)}, u32[]{:S(2)}) collective-permute-start(f32[2,128,128]{2,1,0:T(8,128)} %own.3), channel_id=1, source_target_pairs={{15,0},{2,1},{1,2},{6,5},{5,6},{8,7},{7,8},{10,9},{9,10},{14,13},{... | collective-permute-start | bytes 393224 | tf_op jit(solution)/shard_map/ppermute | solution.py:315
  10.6 1.6 %copy-start = (f32[2,128,128]{2,1,0:T(8,128)S(1)}, f32[2,128,128]{2,1,0:T(8,128)}, u32[]{:S(2)}) copy-start(f32[2,128,128]{2,1,0:T(8,128)} %own.3) | copy-start | bytes 393220
  10.6 1.6 %collective-permute-start.4 = (f32[2,128,128]{2,1,0:T(8,128)S(1)}, f32[2,128,128]{2,1,0:T(8,128)S(1)}, u32[]{:S(2)}, u32[]{:S(2)}) collective-permute-start(f32[2,128,128]{2,1,0:T(8,128)S(1)} %collective-permute-done.1.partner), channel_id=1, source_target_pairs={{0,1},{1,0},{2,3},{3,2},{4,5},{5,4},{6,7},{7,6},{8,9},{9,8},{10,11... | collective-permute-start | bytes 393224 | tf_op jit(solution)/shard_map/ppermute | solution.py:316
